TPU v7x, 128 devices: a whole 4x4x4 slice. The times are simulated.
128 devices in a mesh: blk: 32 (over y_hi, x, z), uly: 4 (over y_lo, core).
Axes of the slice: x: 4, y: 4 (y_hi: 2, y_lo: 2; y = y_hi * 2 + y_lo), z: 4, core: 2. Of those that a mesh axis runs over, the one named last changes fastest.
Arguments:
- cond_query: bfloat16 [6144, 2560], P('blk', 'uly'), may hold values from -100 to 100
- cond_kv: bfloat16 [2, 6144, 2560], P(None, 'blk', 'uly'), may hold values from -100 to 100
- uncond_qkv: bfloat16 [3, 6144, 2560], P(None, ('blk', 'uly')), may hold values from -100 to 100
- uncond_cache: bfloat16 [6144, 2560], P(('blk', 'uly')), may hold values from -2 to 2
- refresh: int32 [6144], P(('blk', 'uly')), may hold values 0 or 1
- valid: int32 [32], replicated, may hold values from 48 to 192, as said below
Outputs:
- guided: bfloat16 [6144, 2560], P(('blk', 'uly'))
- new_cache: bfloat16 [6144, 2560], P(('blk', 'uly'))
Inputs may be any that keep to these rules, and one draw needn't show every extreme that they name: `valid`: every shard holds at least a quarter of its slots; some shard is full in every draw.
All inputs are finite; a program needn't handle non-finite values. No bound on the sum of `refresh` on one device may be relied on, other than what follows from the above.
Results may differ from a plain program's by a relative error of at most 0.012.
Values may be sent and summed in bfloat16 or wider, within the bound.
A program may use at most 192 MiB of HBM per device.

v0:
```python
import jax
import jax.numpy as jnp
from jax import lax
from jax.sharding import PartitionSpec as P

HD = 128


guidance = 5.0


def shifted(block, axis, distance):
    devices = range(lax.axis_size(axis))
    route = [((i - distance) % len(devices), i) for i in devices]
    return lax.ppermute(block, axis, route)


def start_state(queries):
    query_rows = queries.shape[0]
    groups = queries.shape[1] // HD
    return (
        jnp.full((groups, query_rows), -jnp.inf, jnp.float32),
        jnp.zeros((groups, query_rows), jnp.float32),
        jnp.zeros((query_rows, groups, HD), jnp.float32),
    )


def absorb_range(softmax_state, queries, kv_block, usable):
    running_max, denominator, summed = softmax_state
    query_rows = queries.shape[0]
    key_rows = kv_block.shape[1]
    groups = queries.shape[1] // HD
    query_heads = queries.reshape(query_rows, groups, HD)
    key_heads = kv_block[0].reshape(key_rows, groups, HD)
    value_heads = kv_block[1].reshape(key_rows, groups, HD)
    scores = jnp.einsum(
        "qhd,khd->hqk", query_heads, key_heads, preferred_element_type=jnp.float32
    ) * HD ** (-0.5)
    scores = jnp.where(usable, scores, -1e30)
    fresh_max = jnp.maximum(running_max, jnp.max(scores, axis=2))
    rescale = jnp.exp(running_max - fresh_max)
    weights = jnp.where(usable, jnp.exp(scores - fresh_max[:, :, None]), 0.0)
    denominator = denominator * rescale + jnp.sum(weights, axis=2)
    product = jnp.einsum(
        "hqk,khd->qhd",
        weights.astype(jnp.bfloat16),
        value_heads,
        preferred_element_type=jnp.float32,
    )
    summed = summed * jnp.transpose(rescale)[:, :, None] + product
    return (fresh_max, denominator, summed)


def counted(key_rows, valid_count):
    return jnp.arange(key_rows, dtype=jnp.int32) < valid_count


def absorb(softmax_state, queries, kv_block, valid_count):
    return absorb_range(softmax_state, queries, kv_block, counted(kv_block.shape[1], valid_count))


def update(states, queries, blocks, valid_count):
    return tuple(
        (
            absorb(states[branch], queries[branch], blocks, valid_count)
            for branch in range(len(queries))
        )
    )


def finish(softmax_state):
    running_max, denominator, summed = softmax_state
    normed = summed / jnp.transpose(denominator)[:, :, None]
    return normed.reshape(summed.shape[0], -1).astype(jnp.bfloat16)


def circulate(queries, blocks, valid):
    shards = lax.axis_size("blk")
    position = lax.axis_index("blk")
    states = tuple((start_state(query_block) for query_block in queries))
    states = update(states, queries, blocks, valid[position])

    def step_forward(offset, loop_state):
        held, moving = loop_state
        moving = shifted(moving, "blk", 1)
        held = update(held, queries, moving, valid[(position - offset) % shards])
        return (held, moving)

    states, moving = lax.fori_loop(1, shards, step_forward, (states, blocks))
    return tuple((finish(held) for held in states))


def attend(queries, blocks, valid):
    return circulate(queries, blocks, valid)


def on_device(cond_query, cond_kv, uncond_qkv, uncond_cache, refresh, valid):
    head_layout = lax.all_to_all(uncond_qkv, "uly", split_axis=2, concat_axis=1, tiled=True)
    fresh_query = head_layout[0]
    fresh_kv = head_layout[1:]
    conditional = attend((cond_query,), cond_kv, valid)[0]
    fresh = attend((fresh_query,), fresh_kv, valid)[0]
    cond_tokens, fresh_tokens = (
        lax.all_to_all(conditional, "uly", split_axis=0, concat_axis=1, tiled=True),
        lax.all_to_all(fresh, "uly", split_axis=0, concat_axis=1, tiled=True),
    )
    new_cache = jnp.where(refresh[:, None] == 1, fresh_tokens, uncond_cache)
    chosen = new_cache.astype(jnp.float32)
    guided = (chosen + guidance * (cond_tokens.astype(jnp.float32) - chosen)).astype(jnp.bfloat16)
    return (guided, new_cache)


def solution(mesh):
    placed = (
        P("blk", "uly"),
        P(None, "blk", "uly"),
        P(None, ("blk", "uly"), None),
        P(("blk", "uly"), None),
        P(("blk", "uly")),
        P(),
    )
    return jax.shard_map(
        on_device,
        mesh=mesh,
        in_specs=placed,
        out_specs=(P(("blk", "uly"), None), P(("blk", "uly"), None)),
        check_vma=False,
    )
```

profile of v0, /device:TPU:1, one launch (start us, length us, event | category | flops | bytes accessed | tf_op | source)
XLA Modules:
  0.0 1211.0 jit_solution(8207872603383142378)
XLA Ops:
  40.2 560.6 %while.42 = (s32[]{:T(128)}, f32[5,192]{1,0:T(8,128)S(1)}, f32[5,192]{1,0:T(8,128)S(1)}, f32[192,5,128]{2,0,1:T(8,128)S(1)}, bf16[2,192,640]{2,1,0:T(8,128)(2,1)...) while((s32[]{:T(128)}, f32[5,192]{1,0:T(8,128)S(1)}, ...), condition=%wide.region_5.6_spmd, body=%wide.region_2.5_spmd.sunk | while | flops 96279568 | bytes 8911240 | solution.py:89
  43.9 15.8 %collective-permute-done = bf16[2,192,640]{2,1,0:T(8,128)(2,1)S(1)} collective-permute-done((bf16[2,192,640]{2,1,0:T(8,128)(2,1)S(1)}, bf16[2,192,640]{2,1,0:T(8,128)(2,1)S(1)}, u32[]{:S(2)}, u32[]{:S(2)}) %collective-permute-start) | collective-permute-done | bytes 491552 | tf_op jit(solution)/shard_map/while/body/eval_jaxpr/ppermute | solution.py:15
  64.7 15.0 %collective-permute-done = bf16[2,192,640]{2,1,0:T(8,128)(2,1)S(1)} collective-permute-done((bf16[2,192,640]{2,1,0:T(8,128)(2,1)S(1)}, bf16[2,192,640]{2,1,0:T(8,128)(2,1)S(1)}, u32[]{:S(2)}, u32[]{:S(2)}) %collective-permute-start) | collective-permute-done | bytes 491552 | tf_op jit(solution)/shard_map/while/body/eval_jaxpr/ppermute | solution.py:15
  84.8 14.1 %collective-permute-done = bf16[2,192,640]{2,1,0:T(8,128)(2,1)S(1)} collective-permute-done((bf16[2,192,640]{2,1,0:T(8,128)(2,1)S(1)}, bf16[2,192,640]{2,1,0:T(8,128)(2,1)S(1)}, u32[]{:S(2)}, u32[]{:S(2)}) %collective-permute-start) | collective-permute-done | bytes 491552 | tf_op jit(solution)/shard_map/while/body/eval_jaxpr/ppermute | solution.py:15
  273.3 13.7 %collective-permute-done = bf16[2,192,640]{2,1,0:T(8,128)(2,1)S(1)} collective-permute-done((bf16[2,192,640]{2,1,0:T(8,128)(2,1)S(1)}, bf16[2,192,640]{2,1,0:T(8,128)(2,1)S(1)}, u32[]{:S(2)}, u32[]{:S(2)}) %collective-permute-start) | collective-permute-done | bytes 491552 | tf_op jit(solution)/shard_map/while/body/eval_jaxpr/ppermute | solution.py:15
  292.0 14.8 %collective-permute-done = bf16[2,192,640]{2,1,0:T(8,128)(2,1)S(1)} collective-permute-done((bf16[2,192,640]{2,1,0:T(8,128)(2,1)S(1)}, bf16[2,192,640]{2,1,0:T(8,128)(2,1)S(1)}, u32[]{:S(2)}, u32[]{:S(2)}) %collective-permute-start) | collective-permute-done | bytes 491552 | tf_op jit(solution)/shard_map/while/body/eval_jaxpr/ppermute | solution.py:15
  311.9 15.9 %collective-permute-done = bf16[2,192,640]{2,1,0:T(8,128)(2,1)S(1)} collective-permute-done((bf16[2,192,640]{2,1,0:T(8,128)(2,1)S(1)}, bf16[2,192,640]{2,1,0:T(8,128)(2,1)S(1)}, u32[]{:S(2)}, u32[]{:S(2)}) %collective-permute-start) | collective-permute-done | bytes 491552 | tf_op jit(solution)/shard_map/while/body/eval_jaxpr/ppermute | solution.py:15
  332.9 16.7 %collective-permute-done = bf16[2,192,640]{2,1,0:T(8,128)(2,1)S(1)} collective-permute-done((bf16[2,192,640]{2,1,0:T(8,128)(2,1)S(1)}, bf16[2,192,640]{2,1,0:T(8,128)(2,1)S(1)}, u32[]{:S(2)}, u32[]{:S(2)}) %collective-permute-start) | collective-permute-done | bytes 491552 | tf_op jit(solution)/shard_map/while/body/eval_jaxpr/ppermute | solution.py:15
  354.7 15.8 %collective-permute-done = bf16[2,192,640]{2,1,0:T(8,128)(2,1)S(1)} collective-permute-done((bf16[2,192,640]{2,1,0:T(8,128)(2,1)S(1)}, bf16[2,192,640]{2,1,0:T(8,128)(2,1)S(1)}, u32[]{:S(2)}, u32[]{:S(2)}) %collective-permute-start) | collective-permute-done | bytes 491552 | tf_op jit(solution)/shard_map/while/body/eval_jaxpr/ppermute | solution.py:15
  375.6 14.9 %collective-permute-done = bf16[2,192,640]{2,1,0:T(8,128)(2,1)S(1)} collective-permute-done((bf16[2,192,640]{2,1,0:T(8,128)(2,1)S(1)}, bf16[2,192,640]{2,1,0:T(8,128)(2,1)S(1)}, u32[]{:S(2)}, u32[]{:S(2)}) %collective-permute-start) | collective-permute-done | bytes 491552 | tf_op jit(solution)/shard_map/while/body/eval_jaxpr/ppermute | solution.py:15
  395.6 14.0 %collective-permute-done = bf16[2,192,640]{2,1,0:T(8,128)(2,1)S(1)} collective-permute-done((bf16[2,192,640]{2,1,0:T(8,128)(2,1)S(1)}, bf16[2,192,640]{2,1,0:T(8,128)(2,1)S(1)}, u32[]{:S(2)}, u32[]{:S(2)}) %collective-permute-start) | collective-permute-done | bytes 491552 | tf_op jit(solution)/shard_map/while/body/eval_jaxpr/ppermute | solution.py:15
  583.8 13.9 %collective-permute-done = bf16[2,192,640]{2,1,0:T(8,128)(2,1)S(1)} collective-permute-done((bf16[2,192,640]{2,1,0:T(8,128)(2,1)S(1)}, bf16[2,192,640]{2,1,0:T(8,128)(2,1)S(1)}, u32[]{:S(2)}, u32[]{:S(2)}) %collective-permute-start) | collective-permute-done | bytes 491552 | tf_op jit(solution)/shard_map/while/body/eval_jaxpr/ppermute | solution.py:15
  602.2 36.5 %all-to-all-start.1 = ((bf16[4,48,640]{2,1,0:T(8,128)(2,1)}), bf16[4,48,640]{2,1,0:T(8,128)(2,1)S(1)}, u32[]{:S(2)}, u32[]{:S(2)}) async-start(bf16[4,48,640]{2,1,0:T(8,128)(2,1)} %convert_element_type.57), calls=%async_computation.1 | async-start | bytes 491520 | tf_op jit(solution)/shard_map/all_to_all | solution.py:105
  640.2 527.2 %while.43 = (s32[]{:T(128)}, f32[5,192]{1,0:T(8,128)S(1)}, f32[5,192]{1,0:T(8,128)S(1)}, f32[192,5,128]{2,0,1:T(8,128)S(1)}, bf16[2,192,640]{2,1,0:T(8,128)(2,1)...) while((s32[]{:T(128)}, f32[5,192]{1,0:T(8,128)S(1)}, ...), condition=%wide.region_11.12_spmd, body=%wide.region_8.11_spmd.sunk | while | flops 96279568 | bytes 8909896 | solution.py:89
  641.5 17.0 %collective-permute-done.1 = bf16[2,192,640]{2,1,0:T(8,128)(2,1)S(1)} collective-permute-done((bf16[2,192,640]{2,1,0:T(8,128)(2,1)S(1)}, bf16[2,192,640]{2,1,0:T(8,128)(2,1)S(1)}, u32[]{:S(2)}, u32[]{:S(2)}) %collective-permute-start.1) | collective-permute-done | bytes 491552 | tf_op jit(solution)/shard_map/while/body/eval_jaxpr/ppermute | solution.py:15
  661.6 16.1 %collective-permute-done.1 = bf16[2,192,640]{2,1,0:T(8,128)(2,1)S(1)} collective-permute-done((bf16[2,192,640]{2,1,0:T(8,128)(2,1)S(1)}, bf16[2,192,640]{2,1,0:T(8,128)(2,1)S(1)}, u32[]{:S(2)}, u32[]{:S(2)}) %collective-permute-start.1) | collective-permute-done | bytes 491552 | tf_op jit(solution)/shard_map/while/body/eval_jaxpr/ppermute | solution.py:15
  680.7 15.2 %collective-permute-done.1 = bf16[2,192,640]{2,1,0:T(8,128)(2,1)S(1)} collective-permute-done((bf16[2,192,640]{2,1,0:T(8,128)(2,1)S(1)}, bf16[2,192,640]{2,1,0:T(8,128)(2,1)S(1)}, u32[]{:S(2)}, u32[]{:S(2)}) %collective-permute-start.1) | collective-permute-done | bytes 491552 | tf_op jit(solution)/shard_map/while/body/eval_jaxpr/ppermute | solution.py:15
  699.0 14.3 %collective-permute-done.1 = bf16[2,192,640]{2,1,0:T(8,128)(2,1)S(1)} collective-permute-done((bf16[2,192,640]{2,1,0:T(8,128)(2,1)S(1)}, bf16[2,192,640]{2,1,0:T(8,128)(2,1)S(1)}, u32[]{:S(2)}, u32[]{:S(2)}) %collective-permute-start.1) | collective-permute-done | bytes 491552 | tf_op jit(solution)/shard_map/while/body/eval_jaxpr/ppermute | solution.py:15
  716.3 13.3 %collective-permute-done.1 = bf16[2,192,640]{2,1,0:T(8,128)(2,1)S(1)} collective-permute-done((bf16[2,192,640]{2,1,0:T(8,128)(2,1)S(1)}, bf16[2,192,640]{2,1,0:T(8,128)(2,1)S(1)}, u32[]{:S(2)}, u32[]{:S(2)}) %collective-permute-start.1) | collective-permute-done | bytes 491552 | tf_op jit(solution)/shard_map/while/body/eval_jaxpr/ppermute | solution.py:15
  839.9 14.3 %collective-permute-done.1 = bf16[2,192,640]{2,1,0:T(8,128)(2,1)S(1)} collective-permute-done((bf16[2,192,640]{2,1,0:T(8,128)(2,1)S(1)}, bf16[2,192,640]{2,1,0:T(8,128)(2,1)S(1)}, u32[]{:S(2)}, u32[]{:S(2)}) %collective-permute-start.1) | collective-permute-done | bytes 491552 | tf_op jit(solution)/shard_map/while/body/eval_jaxpr/ppermute | solution.py:15
  857.3 15.4 %collective-permute-done.1 = bf16[2,192,640]{2,1,0:T(8,128)(2,1)S(1)} collective-permute-done((bf16[2,192,640]{2,1,0:T(8,128)(2,1)S(1)}, bf16[2,192,640]{2,1,0:T(8,128)(2,1)S(1)}, u32[]{:S(2)}, u32[]{:S(2)}) %collective-permute-start.1) | collective-permute-done | bytes 491552 | tf_op jit(solution)/shard_map/while/body/eval_jaxpr/ppermute | solution.py:15
  875.7 16.5 %collective-permute-done.1 = bf16[2,192,640]{2,1,0:T(8,128)(2,1)S(1)} collective-permute-done((bf16[2,192,640]{2,1,0:T(8,128)(2,1)S(1)}, bf16[2,192,640]{2,1,0:T(8,128)(2,1)S(1)}, u32[]{:S(2)}, u32[]{:S(2)}) %collective-permute-start.1) | collective-permute-done | bytes 491552 | tf_op jit(solution)/shard_map/while/body/eval_jaxpr/ppermute | solution.py:15
  895.2 17.4 %collective-permute-done.1 = bf16[2,192,640]{2,1,0:T(8,128)(2,1)S(1)} collective-permute-done((bf16[2,192,640]{2,1,0:T(8,128)(2,1)S(1)}, bf16[2,192,640]{2,1,0:T(8,128)(2,1)S(1)}, u32[]{:S(2)}, u32[]{:S(2)}) %collective-permute-start.1) | collective-permute-done | bytes 491552 | tf_op jit(solution)/shard_map/while/body/eval_jaxpr/ppermute | solution.py:15
  915.7 16.6 %collective-permute-done.1 = bf16[2,192,640]{2,1,0:T(8,128)(2,1)S(1)} collective-permute-done((bf16[2,192,640]{2,1,0:T(8,128)(2,1)S(1)}, bf16[2,192,640]{2,1,0:T(8,128)(2,1)S(1)}, u32[]{:S(2)}, u32[]{:S(2)}) %collective-permute-start.1) | collective-permute-done | bytes 491552 | tf_op jit(solution)/shard_map/while/body/eval_jaxpr/ppermute | solution.py:15
  935.3 15.6 %collective-permute-done.1 = bf16[2,192,640]{2,1,0:T(8,128)(2,1)S(1)} collective-permute-done((bf16[2,192,640]{2,1,0:T(8,128)(2,1)S(1)}, bf16[2,192,640]{2,1,0:T(8,128)(2,1)S(1)}, u32[]{:S(2)}, u32[]{:S(2)}) %collective-permute-start.1) | collective-permute-done | bytes 491552 | tf_op jit(solution)/shard_map/while/body/eval_jaxpr/ppermute | solution.py:15
  954.0 14.7 %collective-permute-done.1 = bf16[2,192,640]{2,1,0:T(8,128)(2,1)S(1)} collective-permute-done((bf16[2,192,640]{2,1,0:T(8,128)(2,1)S(1)}, bf16[2,192,640]{2,1,0:T(8,128)(2,1)S(1)}, u32[]{:S(2)}, u32[]{:S(2)}) %collective-permute-start.1) | collective-permute-done | bytes 491552 | tf_op jit(solution)/shard_map/while/body/eval_jaxpr/ppermute | solution.py:15
  971.7 13.8 %collective-permute-done.1 = bf16[2,192,640]{2,1,0:T(8,128)(2,1)S(1)} collective-permute-done((bf16[2,192,640]{2,1,0:T(8,128)(2,1)S(1)}, bf16[2,192,640]{2,1,0:T(8,128)(2,1)S(1)}, u32[]{:S(2)}, u32[]{:S(2)}) %collective-permute-start.1) | collective-permute-done | bytes 491552 | tf_op jit(solution)/shard_map/while/body/eval_jaxpr/ppermute | solution.py:15
  1095.8 13.6 %collective-permute-done.1 = bf16[2,192,640]{2,1,0:T(8,128)(2,1)S(1)} collective-permute-done((bf16[2,192,640]{2,1,0:T(8,128)(2,1)S(1)}, bf16[2,192,640]{2,1,0:T(8,128)(2,1)S(1)}, u32[]{:S(2)}, u32[]{:S(2)}) %collective-permute-start.1) | collective-permute-done | bytes 491552 | tf_op jit(solution)/shard_map/while/body/eval_jaxpr/ppermute | solution.py:15
  1112.4 14.7 %collective-permute-done.1 = bf16[2,192,640]{2,1,0:T(8,128)(2,1)S(1)} collective-permute-done((bf16[2,192,640]{2,1,0:T(8,128)(2,1)S(1)}, bf16[2,192,640]{2,1,0:T(8,128)(2,1)S(1)}, u32[]{:S(2)}, u32[]{:S(2)}) %collective-permute-start.1) | collective-permute-done | bytes 491552 | tf_op jit(solution)/shard_map/while/body/eval_jaxpr/ppermute | solution.py:15
  1130.1 15.7 %collective-permute-done.1 = bf16[2,192,640]{2,1,0:T(8,128)(2,1)S(1)} collective-permute-done((bf16[2,192,640]{2,1,0:T(8,128)(2,1)S(1)}, bf16[2,192,640]{2,1,0:T(8,128)(2,1)S(1)}, u32[]{:S(2)}, u32[]{:S(2)}) %collective-permute-start.1) | collective-permute-done | bytes 491552 | tf_op jit(solution)/shard_map/while/body/eval_jaxpr/ppermute | solution.py:15
  1148.9 16.8 %collective-permute-done.1 = bf16[2,192,640]{2,1,0:T(8,128)(2,1)S(1)} collective-permute-done((bf16[2,192,640]{2,1,0:T(8,128)(2,1)S(1)}, bf16[2,192,640]{2,1,0:T(8,128)(2,1)S(1)}, u32[]{:S(2)}, u32[]{:S(2)}) %collective-permute-start.1) | collective-permute-done | bytes 491552 | tf_op jit(solution)/shard_map/while/body/eval_jaxpr/ppermute | solution.py:15
  1168.8 36.2 %all-to-all-start.2 = ((bf16[4,48,640]{2,1,0:T(8,128)(2,1)}), bf16[4,48,640]{2,1,0:T(8,128)(2,1)S(1)}, u32[]{:S(2)}, u32[]{:S(2)}) async-start(bf16[4,48,640]{2,1,0:T(8,128)(2,1)} %convert_element_type.61), calls=%async_computation.2 | async-start | bytes 491520 | tf_op jit(solution)/shard_map/all_to_all | solution.py:104
  (1022 shorter events, 704.4 us)
Async XLA Ops:
  8.5 16.1 %all-to-all-start = ((bf16[4,2,46080]{2,1,0:T(2,128)(2,1)}), bf16[4,2,46080]{2,1,0:T(2,128)(2,1)}, u32[]{:S(2)}, u32[]{:S(2)}) async-start(bf16[4,2,46080]{2,1,0:T(2,128)(2,1)} %reshape.52), calls=%async_computation | async-start | bytes 1474560 | tf_op jit(solution)/shard_map/all_to_all | solution.py:98
  40.2 19.5 %collective-permute-start = (bf16[2,192,640]{2,1,0:T(8,128)(2,1)S(1)}, bf16[2,192,640]{2,1,0:T(8,128)(2,1)S(1)}, u32[]{:S(2)}, u32[]{:S(2)}) collective-permute-start(bf16[2,192,640]{2,1,0:T(8,128)(2,1)S(1)} %get-tuple-element.699), channel_id=1, source_target_pairs={{124,0},{0,4},{4,8},{8,12},{12,16},{16,20},{20,24},{24,28},{28,32}... | collective-permute-start | bytes 1474568 | tf_op jit(solution)/shard_map/while/body/eval_jaxpr/ppermute | solution.py:15
  62.7 17.0 %collective-permute-start = (bf16[2,192,640]{2,1,0:T(8,128)(2,1)S(1)}, bf16[2,192,640]{2,1,0:T(8,128)(2,1)S(1)}, u32[]{:S(2)}, u32[]{:S(2)}) collective-permute-start(bf16[2,192,640]{2,1,0:T(8,128)(2,1)S(1)} %get-tuple-element.699), channel_id=1, source_target_pairs={{124,0},{0,4},{4,8},{8,12},{12,16},{16,20},{20,24},{24,28},{28,32}... | collective-permute-start | bytes 1474568 | tf_op jit(solution)/shard_map/while/body/eval_jaxpr/ppermute | solution.py:15
  82.8 16.1 %collective-permute-start = (bf16[2,192,640]{2,1,0:T(8,128)(2,1)S(1)}, bf16[2,192,640]{2,1,0:T(8,128)(2,1)S(1)}, u32[]{:S(2)}, u32[]{:S(2)}) collective-permute-start(bf16[2,192,640]{2,1,0:T(8,128)(2,1)S(1)} %get-tuple-element.699), channel_id=1, source_target_pairs={{124,0},{0,4},{4,8},{8,12},{12,16},{16,20},{20,24},{24,28},{28,32}... | collective-permute-start | bytes 1474568 | tf_op jit(solution)/shard_map/while/body/eval_jaxpr/ppermute | solution.py:15
  102.0 15.2 %collective-permute-start = (bf16[2,192,640]{2,1,0:T(8,128)(2,1)S(1)}, bf16[2,192,640]{2,1,0:T(8,128)(2,1)S(1)}, u32[]{:S(2)}, u32[]{:S(2)}) collective-permute-start(bf16[2,192,640]{2,1,0:T(8,128)(2,1)S(1)} %get-tuple-element.699), channel_id=1, source_target_pairs={{124,0},{0,4},{4,8},{8,12},{12,16},{16,20},{20,24},{24,28},{28,32}... | collective-permute-start | bytes 1474568 | tf_op jit(solution)/shard_map/while/body/eval_jaxpr/ppermute | solution.py:15
  271.2 15.7 %collective-permute-start = (bf16[2,192,640]{2,1,0:T(8,128)(2,1)S(1)}, bf16[2,192,640]{2,1,0:T(8,128)(2,1)S(1)}, u32[]{:S(2)}, u32[]{:S(2)}) collective-permute-start(bf16[2,192,640]{2,1,0:T(8,128)(2,1)S(1)} %get-tuple-element.699), channel_id=1, source_target_pairs={{124,0},{0,4},{4,8},{8,12},{12,16},{16,20},{20,24},{24,28},{28,32}... | collective-permute-start | bytes 1474568 | tf_op jit(solution)/shard_map/while/body/eval_jaxpr/ppermute | solution.py:15
  290.0 16.8 %collective-permute-start = (bf16[2,192,640]{2,1,0:T(8,128)(2,1)S(1)}, bf16[2,192,640]{2,1,0:T(8,128)(2,1)S(1)}, u32[]{:S(2)}, u32[]{:S(2)}) collective-permute-start(bf16[2,192,640]{2,1,0:T(8,128)(2,1)S(1)} %get-tuple-element.699), channel_id=1, source_target_pairs={{124,0},{0,4},{4,8},{8,12},{12,16},{16,20},{20,24},{24,28},{28,32}... | collective-permute-start | bytes 1474568 | tf_op jit(solution)/shard_map/while/body/eval_jaxpr/ppermute | solution.py:15
  309.9 17.9 %collective-permute-start = (bf16[2,192,640]{2,1,0:T(8,128)(2,1)S(1)}, bf16[2,192,640]{2,1,0:T(8,128)(2,1)S(1)}, u32[]{:S(2)}, u32[]{:S(2)}) collective-permute-start(bf16[2,192,640]{2,1,0:T(8,128)(2,1)S(1)} %get-tuple-element.699), channel_id=1, source_target_pairs={{124,0},{0,4},{4,8},{8,12},{12,16},{16,20},{20,24},{24,28},{28,32}... | collective-permute-start | bytes 1474568 | tf_op jit(solution)/shard_map/while/body/eval_jaxpr/ppermute | solution.py:15
  330.9 18.7 %collective-permute-start = (bf16[2,192,640]{2,1,0:T(8,128)(2,1)S(1)}, bf16[2,192,640]{2,1,0:T(8,128)(2,1)S(1)}, u32[]{:S(2)}, u32[]{:S(2)}) collective-permute-start(bf16[2,192,640]{2,1,0:T(8,128)(2,1)S(1)} %get-tuple-element.699), channel_id=1, source_target_pairs={{124,0},{0,4},{4,8},{8,12},{12,16},{16,20},{20,24},{24,28},{28,32}... | collective-permute-start | bytes 1474568 | tf_op jit(solution)/shard_map/while/body/eval_jaxpr/ppermute | solution.py:15
  352.7 17.8 %collective-permute-start = (bf16[2,192,640]{2,1,0:T(8,128)(2,1)S(1)}, bf16[2,192,640]{2,1,0:T(8,128)(2,1)S(1)}, u32[]{:S(2)}, u32[]{:S(2)}) collective-permute-start(bf16[2,192,640]{2,1,0:T(8,128)(2,1)S(1)} %get-tuple-element.699), channel_id=1, source_target_pairs={{124,0},{0,4},{4,8},{8,12},{12,16},{16,20},{20,24},{24,28},{28,32}... | collective-permute-start | bytes 1474568 | tf_op jit(solution)/shard_map/while/body/eval_jaxpr/ppermute | solution.py:15
  373.6 16.9 %collective-permute-start = (bf16[2,192,640]{2,1,0:T(8,128)(2,1)S(1)}, bf16[2,192,640]{2,1,0:T(8,128)(2,1)S(1)}, u32[]{:S(2)}, u32[]{:S(2)}) collective-permute-start(bf16[2,192,640]{2,1,0:T(8,128)(2,1)S(1)} %get-tuple-element.699), channel_id=1, source_target_pairs={{124,0},{0,4},{4,8},{8,12},{12,16},{16,20},{20,24},{24,28},{28,32}... | collective-permute-start | bytes 1474568 | tf_op jit(solution)/shard_map/while/body/eval_jaxpr/ppermute | solution.py:15
  393.5 16.0 %collective-permute-start = (bf16[2,192,640]{2,1,0:T(8,128)(2,1)S(1)}, bf16[2,192,640]{2,1,0:T(8,128)(2,1)S(1)}, u32[]{:S(2)}, u32[]{:S(2)}) collective-permute-start(bf16[2,192,640]{2,1,0:T(8,128)(2,1)S(1)} %get-tuple-element.699), channel_id=1, source_target_pairs={{124,0},{0,4},{4,8},{8,12},{12,16},{16,20},{20,24},{24,28},{28,32}... | collective-permute-start | bytes 1474568 | tf_op jit(solution)/shard_map/while/body/eval_jaxpr/ppermute | solution.py:15
  412.6 15.1 %collective-permute-start = (bf16[2,192,640]{2,1,0:T(8,128)(2,1)S(1)}, bf16[2,192,640]{2,1,0:T(8,128)(2,1)S(1)}, u32[]{:S(2)}, u32[]{:S(2)}) collective-permute-start(bf16[2,192,640]{2,1,0:T(8,128)(2,1)S(1)} %get-tuple-element.699), channel_id=1, source_target_pairs={{124,0},{0,4},{4,8},{8,12},{12,16},{16,20},{20,24},{24,28},{28,32}... | collective-permute-start | bytes 1474568 | tf_op jit(solution)/shard_map/while/body/eval_jaxpr/ppermute | solution.py:15
  581.8 15.9 %collective-permute-start = (bf16[2,192,640]{2,1,0:T(8,128)(2,1)S(1)}, bf16[2,192,640]{2,1,0:T(8,128)(2,1)S(1)}, u32[]{:S(2)}, u32[]{:S(2)}) collective-permute-start(bf16[2,192,640]{2,1,0:T(8,128)(2,1)S(1)} %get-tuple-element.699), channel_id=1, source_target_pairs={{124,0},{0,4},{4,8},{8,12},{12,16},{16,20},{20,24},{24,28},{28,32}... | collective-permute-start | bytes 1474568 | tf_op jit(solution)/shard_map/while/body/eval_jaxpr/ppermute | solution.py:15
  602.2 566.6 %all-to-all-start.1 = ((bf16[4,48,640]{2,1,0:T(8,128)(2,1)}), bf16[4,48,640]{2,1,0:T(8,128)(2,1)S(1)}, u32[]{:S(2)}, u32[]{:S(2)}) async-start(bf16[4,48,640]{2,1,0:T(8,128)(2,1)} %convert_element_type.57), calls=%async_computation.1 | async-start | bytes 491520 | tf_op jit(solution)/shard_map/all_to_all | solution.py:105
  640.2 18.4 %collective-permute-start.1 = (bf16[2,192,640]{2,1,0:T(8,128)(2,1)S(1)}, bf16[2,192,640]{2,1,0:T(8,128)(2,1)S(1)}, u32[]{:S(2)}, u32[]{:S(2)}) collective-permute-start(bf16[2,192,640]{2,1,0:T(8,128)(2,1)S(1)} %get-tuple-element.663), channel_id=1, source_target_pairs={{124,0},{0,4},{4,8},{8,12},{12,16},{16,20},{20,24},{24,28},{28,32}... | collective-permute-start | bytes 1474568 | tf_op jit(solution)/shard_map/while/body/eval_jaxpr/ppermute | solution.py:15
  660.2 17.5 %collective-permute-start.1 = (bf16[2,192,640]{2,1,0:T(8,128)(2,1)S(1)}, bf16[2,192,640]{2,1,0:T(8,128)(2,1)S(1)}, u32[]{:S(2)}, u32[]{:S(2)}) collective-permute-start(bf16[2,192,640]{2,1,0:T(8,128)(2,1)S(1)} %get-tuple-element.663), channel_id=1, source_target_pairs={{124,0},{0,4},{4,8},{8,12},{12,16},{16,20},{20,24},{24,28},{28,32}... | collective-permute-start | bytes 1474568 | tf_op jit(solution)/shard_map/while/body/eval_jaxpr/ppermute | solution.py:15
  679.4 16.5 %collective-permute-start.1 = (bf16[2,192,640]{2,1,0:T(8,128)(2,1)S(1)}, bf16[2,192,640]{2,1,0:T(8,128)(2,1)S(1)}, u32[]{:S(2)}, u32[]{:S(2)}) collective-permute-start(bf16[2,192,640]{2,1,0:T(8,128)(2,1)S(1)} %get-tuple-element.663), channel_id=1, source_target_pairs={{124,0},{0,4},{4,8},{8,12},{12,16},{16,20},{20,24},{24,28},{28,32}... | collective-permute-start | bytes 1474568 | tf_op jit(solution)/shard_map/while/body/eval_jaxpr/ppermute | solution.py:15
  697.6 15.6 %collective-permute-start.1 = (bf16[2,192,640]{2,1,0:T(8,128)(2,1)S(1)}, bf16[2,192,640]{2,1,0:T(8,128)(2,1)S(1)}, u32[]{:S(2)}, u32[]{:S(2)}) collective-permute-start(bf16[2,192,640]{2,1,0:T(8,128)(2,1)S(1)} %get-tuple-element.663), channel_id=1, source_target_pairs={{124,0},{0,4},{4,8},{8,12},{12,16},{16,20},{20,24},{24,28},{28,32}... | collective-permute-start | bytes 1474568 | tf_op jit(solution)/shard_map/while/body/eval_jaxpr/ppermute | solution.py:15
  838.6 15.7 %collective-permute-start.1 = (bf16[2,192,640]{2,1,0:T(8,128)(2,1)S(1)}, bf16[2,192,640]{2,1,0:T(8,128)(2,1)S(1)}, u32[]{:S(2)}, u32[]{:S(2)}) collective-permute-start(bf16[2,192,640]{2,1,0:T(8,128)(2,1)S(1)} %get-tuple-element.663), channel_id=1, source_target_pairs={{124,0},{0,4},{4,8},{8,12},{12,16},{16,20},{20,24},{24,28},{28,32}... | collective-permute-start | bytes 1474568 | tf_op jit(solution)/shard_map/while/body/eval_jaxpr/ppermute | solution.py:15
  855.9 16.8 %collective-permute-start.1 = (bf16[2,192,640]{2,1,0:T(8,128)(2,1)S(1)}, bf16[2,192,640]{2,1,0:T(8,128)(2,1)S(1)}, u32[]{:S(2)}, u32[]{:S(2)}) collective-permute-start(bf16[2,192,640]{2,1,0:T(8,128)(2,1)S(1)} %get-tuple-element.663), channel_id=1, source_target_pairs={{124,0},{0,4},{4,8},{8,12},{12,16},{16,20},{20,24},{24,28},{28,32}... | collective-permute-start | bytes 1474568 | tf_op jit(solution)/shard_map/while/body/eval_jaxpr/ppermute | solution.py:15
  874.4 17.8 %collective-permute-start.1 = (bf16[2,192,640]{2,1,0:T(8,128)(2,1)S(1)}, bf16[2,192,640]{2,1,0:T(8,128)(2,1)S(1)}, u32[]{:S(2)}, u32[]{:S(2)}) collective-permute-start(bf16[2,192,640]{2,1,0:T(8,128)(2,1)S(1)} %get-tuple-element.663), channel_id=1, source_target_pairs={{124,0},{0,4},{4,8},{8,12},{12,16},{16,20},{20,24},{24,28},{28,32}... | collective-permute-start | bytes 1474568 | tf_op jit(solution)/shard_map/while/body/eval_jaxpr/ppermute | solution.py:15
  893.9 18.8 %collective-permute-start.1 = (bf16[2,192,640]{2,1,0:T(8,128)(2,1)S(1)}, bf16[2,192,640]{2,1,0:T(8,128)(2,1)S(1)}, u32[]{:S(2)}, u32[]{:S(2)}) collective-permute-start(bf16[2,192,640]{2,1,0:T(8,128)(2,1)S(1)} %get-tuple-element.663), channel_id=1, source_target_pairs={{124,0},{0,4},{4,8},{8,12},{12,16},{16,20},{20,24},{24,28},{28,32}... | collective-permute-start | bytes 1474568 | tf_op jit(solution)/shard_map/while/body/eval_jaxpr/ppermute | solution.py:15
  914.3 17.9 %collective-permute-start.1 = (bf16[2,192,640]{2,1,0:T(8,128)(2,1)S(1)}, bf16[2,192,640]{2,1,0:T(8,128)(2,1)S(1)}, u32[]{:S(2)}, u32[]{:S(2)}) collective-permute-start(bf16[2,192,640]{2,1,0:T(8,128)(2,1)S(1)} %get-tuple-element.663), channel_id=1, source_target_pairs={{124,0},{0,4},{4,8},{8,12},{12,16},{16,20},{20,24},{24,28},{28,32}... | collective-permute-start | bytes 1474568 | tf_op jit(solution)/shard_map/while/body/eval_jaxpr/ppermute | solution.py:15
  933.9 17.0 %collective-permute-start.1 = (bf16[2,192,640]{2,1,0:T(8,128)(2,1)S(1)}, bf16[2,192,640]{2,1,0:T(8,128)(2,1)S(1)}, u32[]{:S(2)}, u32[]{:S(2)}) collective-permute-start(bf16[2,192,640]{2,1,0:T(8,128)(2,1)S(1)} %get-tuple-element.663), channel_id=1, source_target_pairs={{124,0},{0,4},{4,8},{8,12},{12,16},{16,20},{20,24},{24,28},{28,32}... | collective-permute-start | bytes 1474568 | tf_op jit(solution)/shard_map/while/body/eval_jaxpr/ppermute | solution.py:15
  952.6 16.1 %collective-permute-start.1 = (bf16[2,192,640]{2,1,0:T(8,128)(2,1)S(1)}, bf16[2,192,640]{2,1,0:T(8,128)(2,1)S(1)}, u32[]{:S(2)}, u32[]{:S(2)}) collective-permute-start(bf16[2,192,640]{2,1,0:T(8,128)(2,1)S(1)} %get-tuple-element.663), channel_id=1, source_target_pairs={{124,0},{0,4},{4,8},{8,12},{12,16},{16,20},{20,24},{24,28},{28,32}... | collective-permute-start | bytes 1474568 | tf_op jit(solution)/shard_map/while/body/eval_jaxpr/ppermute | solution.py:15
  970.4 15.1 %collective-permute-start.1 = (bf16[2,192,640]{2,1,0:T(8,128)(2,1)S(1)}, bf16[2,192,640]{2,1,0:T(8,128)(2,1)S(1)}, u32[]{:S(2)}, u32[]{:S(2)}) collective-permute-start(bf16[2,192,640]{2,1,0:T(8,128)(2,1)S(1)} %get-tuple-element.663), channel_id=1, source_target_pairs={{124,0},{0,4},{4,8},{8,12},{12,16},{16,20},{20,24},{24,28},{28,32}... | collective-permute-start | bytes 1474568 | tf_op jit(solution)/shard_map/while/body/eval_jaxpr/ppermute | solution.py:15
  1094.5 14.9 %collective-permute-start.1 = (bf16[2,192,640]{2,1,0:T(8,128)(2,1)S(1)}, bf16[2,192,640]{2,1,0:T(8,128)(2,1)S(1)}, u32[]{:S(2)}, u32[]{:S(2)}) collective-permute-start(bf16[2,192,640]{2,1,0:T(8,128)(2,1)S(1)} %get-tuple-element.663), channel_id=1, source_target_pairs={{124,0},{0,4},{4,8},{8,12},{12,16},{16,20},{20,24},{24,28},{28,32}... | collective-permute-start | bytes 1474568 | tf_op jit(solution)/shard_map/while/body/eval_jaxpr/ppermute | solution.py:15
  1111.1 16.0 %collective-permute-start.1 = (bf16[2,192,640]{2,1,0:T(8,128)(2,1)S(1)}, bf16[2,192,640]{2,1,0:T(8,128)(2,1)S(1)}, u32[]{:S(2)}, u32[]{:S(2)}) collective-permute-start(bf16[2,192,640]{2,1,0:T(8,128)(2,1)S(1)} %get-tuple-element.663), channel_id=1, source_target_pairs={{124,0},{0,4},{4,8},{8,12},{12,16},{16,20},{20,24},{24,28},{28,32}... | collective-permute-start | bytes 1474568 | tf_op jit(solution)/shard_map/while/body/eval_jaxpr/ppermute | solution.py:15
  1128.8 17.1 %collective-permute-start.1 = (bf16[2,192,640]{2,1,0:T(8,128)(2,1)S(1)}, bf16[2,192,640]{2,1,0:T(8,128)(2,1)S(1)}, u32[]{:S(2)}, u32[]{:S(2)}) collective-permute-start(bf16[2,192,640]{2,1,0:T(8,128)(2,1)S(1)} %get-tuple-element.663), channel_id=1, source_target_pairs={{124,0},{0,4},{4,8},{8,12},{12,16},{16,20},{20,24},{24,28},{28,32}... | collective-permute-start | bytes 1474568 | tf_op jit(solution)/shard_map/while/body/eval_jaxpr/ppermute | solution.py:15
  1147.5 18.2 %collective-permute-start.1 = (bf16[2,192,640]{2,1,0:T(8,128)(2,1)S(1)}, bf16[2,192,640]{2,1,0:T(8,128)(2,1)S(1)}, u32[]{:S(2)}, u32[]{:S(2)}) collective-permute-start(bf16[2,192,640]{2,1,0:T(8,128)(2,1)S(1)} %get-tuple-element.663), channel_id=1, source_target_pairs={{124,0},{0,4},{4,8},{8,12},{12,16},{16,20},{20,24},{24,28},{28,32}... | collective-permute-start | bytes 1474568 | tf_op jit(solution)/shard_map/while/body/eval_jaxpr/ppermute | solution.py:15
  1168.8 41.2 %all-to-all-start.2 = ((bf16[4,48,640]{2,1,0:T(8,128)(2,1)}), bf16[4,48,640]{2,1,0:T(8,128)(2,1)S(1)}, u32[]{:S(2)}, u32[]{:S(2)}) async-start(bf16[4,48,640]{2,1,0:T(8,128)(2,1)} %convert_element_type.61), calls=%async_computation.2 | async-start | bytes 491520 | tf_op jit(solution)/shard_map/all_to_all | solution.py:104
  (103 other events, 1293.8 us)
where the time goes:
time: 1210 us
  waiting for transfers between devices  846 us (70%)
  other arithmetic  96.5 us (8%)
  local copies, waits for them, and re-layouts  91.6 us (8%)
  starting transfers between devices  84.7 us (7%)
  matrix products  84 us (7%)
    ppermute x62, waiting for transfers between devices, shifted(): return lax.ppermute(block, axis, route)  835 us
    lt x63, other arithmetic, counted(): return jnp.arange(key_rows, dtype=jnp.int32) < valid_count  59.4 us
    dot_general x64, matrix products, absorb_range(): jnp.einsum('qhd,khd->hqk', query_heads, key_heads, preferred_element_type...  46.6 us
    dynamic_slice x62, local copies, waits for them, and re-layouts, step_forward(): held = update(held, queries, moving, valid[(position - offset) % shards])  38.5 us
    dot_general x64, matrix products, absorb_range(): jnp.einsum('hqk,khd->qhd', weights.astype(jnp.bfloat16), value_heads, pre...  37.4 us
    all_to_all x1, starting transfers between devices, on_device(): lax.all_to_all(fresh, 'uly', split_axis=0, concat_axis=1, tiled=True)  36.5 us
    all_to_all x1, starting transfers between devices, on_device(): lax.all_to_all(conditional, 'uly', split_axis=0, concat_axis=1, tiled=True)  36.2 us
    reduce_sum x63, other arithmetic, absorb_range(): denominator = denominator * rescale + jnp.sum(weights, axis=2)  33.9 us
  transfers between devices with their start and end apart: 65, of which 64 were waited for; matrix products, arithmetic and copies ran while one was open for 13% of the time, Pallas kernels for 0%

commit v1 on v0

v1 whole, which is shorter than its diff:
```python
import functools

import jax
import jax.numpy as jnp
from jax import lax
from jax.experimental import pallas as pl
from jax.experimental.pallas import tpu as pltpu
from jax.sharding import PartitionSpec as P

HD = 128
GUIDANCE = 5.0
MESH = pl.DeviceIdType.MESH
LOG2E = 1.4426950408889634
SCALE = LOG2E * HD ** (-0.5)
UNUSABLE = -1e30

HEADS = 5
SHARD = 192
PIECE = 48
PAIR = 2 * SHARD
ALL = 4 * PAIR
TILE = 256
CHUNK = 256
NT = (((1,), (1,)), ((), ()))


def place():
    blk, uly = lax.axis_index("blk"), lax.axis_index("uly")
    return blk // 16, (blk // 4) % 4, blk % 4, uly


def kernel(
    valid_ref, q_hbm, kv_hbm, qkv_hbm, out_ref,
    q_all, kv_all, vt, bias, ones, scores, o_send, o_recv, st_send, st_recv, stage,
    y_ssem, y_rsem, y_lsem, x_ssem, x_rsem, z_ssem, z_rsem, o_ssem, o_rsem, f_ssem, f_rsem, f_lsem,
):
    hi, x, z, uly = place()
    me = hi * 4 + uly
    my_x = pl.multiple_of(x * PAIR, PAIR)
    my_z = pl.multiple_of(z * PAIR, PAIR)

    def column(member):
        return ((member // 4) * 16 + x * 4 + z, member % 4)

    def along_x(step):
        return (hi * 16 + lax.rem(x + step, 4) * 4 + z, uly)

    def along_z(step):
        return (hi * 16 + x * 4 + lax.rem(z + step, 4), uly)

    barrier = pltpu.get_barrier_semaphore()
    for step in range(1, 8):
        pl.semaphore_signal(barrier, inc=1, device_id=column(lax.rem(me + step, 8)), device_id_type=MESH)
    for step in range(1, 4):
        pl.semaphore_signal(barrier, inc=1, device_id=along_x(step), device_id_type=MESH)
        pl.semaphore_signal(barrier, inc=1, device_id=along_z(step), device_id_type=MESH)

    def head_columns(head):
        return pl.ds(head * HD, HD)

    def cond_own(head):
        return (
            pltpu.make_async_copy(
                q_hbm.at[:, head_columns(head)], q_all.at[head, pl.ds(my_z, SHARD)], y_lsem.at[head, 0]),
            pltpu.make_async_copy(
                kv_hbm.at[:, :, head_columns(head)], kv_all.at[head, :, pl.ds(my_x, SHARD)], y_lsem.at[head, 1]),
        )

    def cond_far(head):
        to = column(uly)
        return (
            pltpu.make_async_remote_copy(
                q_hbm.at[:, head_columns(head)], q_all.at[head, pl.ds(my_z + SHARD, SHARD)],
                y_ssem.at[head, 4, 0], y_rsem.at[head, 8, 0], device_id=to, device_id_type=MESH),
            pltpu.make_async_remote_copy(
                kv_hbm.at[:, :, head_columns(head)], kv_all.at[head, :, pl.ds(my_x + SHARD, SHARD)],
                y_ssem.at[head, 4, 1], y_rsem.at[head, 8, 1], device_id=to, device_id_type=MESH),
        )

    def uncond_refs(head, group, source):
        columns = pl.ds(pl.multiple_of((group * HEADS + head) * HD, HD), HD)
        row = pl.multiple_of(source * PIECE, PIECE)
        return (
            (qkv_hbm.at[0, :, columns], q_all.at[head, pl.ds(my_z + row, PIECE)]),
            (qkv_hbm.at[pl.ds(1, 2), :, columns], kv_all.at[head, :, pl.ds(my_x + row, PIECE)]),
        )

    def uncond_own(head):
        return tuple(
            pltpu.make_async_copy(src, dst, y_lsem.at[head, i])
            for i, (src, dst) in enumerate(uncond_refs(head, uly, me)))

    def uncond_far(head, group, source):
        return tuple(
            pltpu.make_async_remote_copy(
                src, dst, y_ssem.at[head, group, i], y_rsem.at[head, source, i],
                device_id=column(4 + group), device_id_type=MESH)
            for i, (src, dst) in enumerate(uncond_refs(head, group, source)))

    def y_start(head):
        @pl.when(hi == 0)
        def _():
            for copy in cond_own(head):
                copy.start()

        @pl.when(hi == 1)
        def _():
            for copy in cond_far(head):
                copy.start()
            for copy in uncond_own(head):
                copy.start()

        for group in range(4):
            @pl.when(me != 4 + group)
            def _():
                for copy in uncond_far(head, group, me):
                    copy.start()

    def y_wait(head):
        @pl.when(hi == 0)
        def _():
            for copy in cond_own(head):
                copy.wait()
            for copy in cond_far(head):
                copy.wait_recv()

        @pl.when(hi == 1)
        def _():
            for copy in uncond_own(head):
                copy.wait()
            for source in range(8):
                @pl.when(me != source)
                def _():
                    for copy in uncond_far(head, 0, source):
                        copy.wait_recv()

    def y_sent(head):
        @pl.when(hi == 1)
        def _():
            for copy in cond_far(head):
                copy.wait_send()

        for group in range(4):
            @pl.when(me != 4 + group)
            def _():
                for copy in uncond_far(head, group, me):
                    copy.wait_send()

    def gathers(head, from_x, from_z):
        copies = []
        for step in (2, 1, 3):
            block = kv_all.at[head, :, pl.ds(from_x(step), PAIR)]
            copies.append(pltpu.make_async_remote_copy(
                block, block, x_ssem.at[head, step - 1], x_rsem.at[head, step - 1],
                device_id=along_x(step), device_id_type=MESH))
            block = q_all.at[head, pl.ds(from_z(step), PAIR)]
            copies.append(pltpu.make_async_remote_copy(
                block, block, z_ssem.at[head, step - 1], z_rsem.at[head, step - 1],
                device_id=along_z(step), device_id_type=MESH))
        return copies

    def gathers_out(head):
        return gathers(head, lambda step: my_x, lambda step: my_z)

    def gathers_in(head):
        return gathers(
            head,
            lambda step: pl.multiple_of(lax.rem(x + 4 - step, 4) * PAIR, PAIR),
            lambda step: pl.multiple_of(lax.rem(z + 4 - step, 4) * PAIR, PAIR))

    def o_copies(head, step):
        lanes = pl.ds(pl.multiple_of(lax.rem(z + step, 4) * PAIR, PAIR), PAIR)
        return (
            pltpu.make_async_remote_copy(
                o_send.at[head, :, lanes], o_recv.at[head, step - 1], o_ssem.at[head, step - 1, 0],
                o_rsem.at[head, step - 1, 0], device_id=along_z(step), device_id_type=MESH),
            pltpu.make_async_remote_copy(
                st_send.at[head, :, lanes], st_recv.at[head, step - 1], o_ssem.at[head, step - 1, 1],
                o_rsem.at[head, step - 1, 1], device_id=along_z(step), device_id_type=MESH),
        )

    def final_refs(head, target, branch, group):
        columns = pl.ds(pl.multiple_of((group * HEADS + head) * HD, HD), HD)
        row = pl.multiple_of(target * PIECE, PIECE)
        return stage.at[head, pl.ds(row, PIECE)], out_ref.at[branch, :, columns]

    def final_own(head):
        src, dst = final_refs(head, me, hi, uly)
        return pltpu.make_async_copy(src, dst, f_lsem.at[head])

    def final_far(head, step):
        target = lax.rem(me + step, 8)
        src, dst = final_refs(head, target, hi, uly)
        return pltpu.make_async_remote_copy(
            src, dst, f_ssem.at[head, step - 1], f_rsem.at[head, step - 1],
            device_id=column(target), device_id_type=MESH)

    def prepare():
        lane = lax.broadcasted_iota(jnp.int32, (SHARD, HD), 1)
        row = lax.broadcasted_iota(jnp.int32, (SHARD, HD), 0)
        for slot in range(4):
            for half in range(2):
                present = valid_ref[half * 16 + slot * 4 + z]
                block = jnp.where((row >= present) & (lane == 0), UNUSABLE, 0.0)
                bias[pl.ds(slot * PAIR + half * SHARD, SHARD), :] = block.astype(jnp.bfloat16)
        ones[...] = jnp.where(
            lax.broadcasted_iota(jnp.int32, (TILE, HD), 1) == 0, 1.0, 0.0).astype(jnp.bfloat16)
        vt[pl.ds(HD, 16), :] = jnp.ones((16, ALL), jnp.bfloat16)

    def transpose_values(head):
        rows = lax.broadcasted_iota(jnp.int32, (HD, HD), 0)
        lanes = lax.broadcasted_iota(jnp.int32, (HD, HD), 1)
        eye = (rows == lanes).astype(jnp.bfloat16)
        for chunk in range(ALL // CHUNK):
            span = pl.ds(chunk * CHUNK, CHUNK)
            vt[pl.ds(0, HD), span] = lax.dot_general(
                eye, kv_all[head, 1, span, :], NT, preferred_element_type=jnp.float32).astype(jnp.bfloat16)

    def tile(head, start):
        start = pl.multiple_of(start, TILE)
        queries = jnp.concatenate([q_all[head, pl.ds(start, TILE), :], ones[...]], axis=1)
        top = None
        for chunk in range(ALL // CHUNK):
            span = pl.ds(chunk * CHUNK, CHUNK)
            keys = jnp.concatenate([kv_all[head, 0, span, :], bias[span, :]], axis=1)
            part = lax.dot_general(keys, queries, NT, preferred_element_type=jnp.float32)
            scores[span, :] = part
            part_top = jnp.max(part, axis=0, keepdims=True)
            top = part_top if top is None else jnp.maximum(top, part_top)
        total = jnp.zeros((HD + 16, TILE), jnp.float32)
        for chunk in range(ALL // CHUNK):
            span = pl.ds(chunk * CHUNK, CHUNK)
            weights = jnp.exp2((scores[span, :] - top) * SCALE).astype(jnp.bfloat16)
            total = total + jnp.dot(vt[:, span], weights, preferred_element_type=jnp.float32)
        o_send[head, :, pl.ds(start, TILE)] = total[:HD].astype(jnp.bfloat16)
        st_send[head, pl.ds(0, 1), pl.ds(start, TILE)] = top
        st_send[head, pl.ds(1, 1), pl.ds(start, TILE)] = total[HD:HD + 1]

    def compute(head):
        transpose_values(head)
        mine = z // 2
        for part in range(2):
            half = 1 - mine if part == 0 else mine

            def body(i, _):
                tile(head, half * (2 * PAIR) + i * TILE)
                return 0

            lax.fori_loop(0, 2 * PAIR // TILE, body, 0)
            for step in range(1, 4):
                target = lax.rem(z + step, 4)

                @pl.when(target // 2 == half)
                def _():
                    for copy in o_copies(head, step):
                        copy.start()

    def merge(head):
        for step in range(1, 4):
            for copy in o_copies(head, step):
                copy.wait_recv()
        own = pl.ds(my_z, PAIR)
        tops = [st_send[head, pl.ds(0, 1), own]] + [st_recv[head, i, pl.ds(0, 1), :] for i in range(3)]
        sums = [st_send[head, pl.ds(1, 1), own]] + [st_recv[head, i, pl.ds(1, 1), :] for i in range(3)]
        parts = [o_send[head, :, own]] + [o_recv[head, i] for i in range(3)]
        top = functools.reduce(jnp.maximum, tops)
        factors = [jnp.exp2((t - top) * SCALE) for t in tops]
        denominator = sum(f * s for f, s in zip(factors, sums))
        numerator = sum(f * p.astype(jnp.float32) for f, p in zip(factors, parts))
        stage[head] = (numerator / denominator).T.astype(jnp.bfloat16)
        final_own(head).start()
        for step in range(1, 8):
            final_far(head, step).start()

    def spread(head):
        y_wait(head)
        for copy in gathers_out(head):
            copy.start()
        if head + 2 < HEADS:
            y_start(head + 2)

    prepare()
    pl.semaphore_wait(barrier, 13)
    y_start(0)
    y_start(1)
    spread(0)
    spread(1)
    for head in range(HEADS):
        for copy in gathers_in(head):
            copy.wait_recv()
        compute(head)
        if head + 2 < HEADS:
            spread(head + 2)
        if head >= 1:
            merge(head - 1)
    merge(HEADS - 1)

    for head in range(HEADS):
        y_sent(head)
        for copy in gathers_out(head):
            copy.wait_send()
        for step in range(1, 4):
            for copy in o_copies(head, step):
                copy.wait_send()
        final_own(head).wait()
        for step in range(1, 8):
            final_far(head, step).wait()


def attend(cond_query, cond_kv, uncond_qkv, valid):
    any_space = pl.BlockSpec(memory_space=pl.ANY)
    dma = pltpu.SemaphoreType.DMA
    return pl.pallas_call(
        kernel,
        out_shape=jax.ShapeDtypeStruct((2, PIECE, 4 * HEADS * HD), jnp.bfloat16),
        in_specs=[pl.BlockSpec(memory_space=pltpu.SMEM), any_space, any_space, any_space],
        out_specs=any_space,
        scratch_shapes=[
            pltpu.VMEM((HEADS, ALL, HD), jnp.bfloat16),
            pltpu.VMEM((HEADS, 2, ALL, HD), jnp.bfloat16),
            pltpu.VMEM((HD + 16, ALL), jnp.bfloat16),
            pltpu.VMEM((ALL, HD), jnp.bfloat16),
            pltpu.VMEM((TILE, HD), jnp.bfloat16),
            pltpu.VMEM((ALL, TILE), jnp.float32),
            pltpu.VMEM((HEADS, HD, ALL), jnp.bfloat16),
            pltpu.VMEM((HEADS, 3, HD, PAIR), jnp.bfloat16),
            pltpu.VMEM((HEADS, 8, ALL), jnp.float32),
            pltpu.VMEM((HEADS, 3, 8, PAIR), jnp.float32),
            pltpu.VMEM((HEADS, PAIR, HD), jnp.bfloat16),
            dma((HEADS, 5, 2)), dma((HEADS, 9, 2)), dma((HEADS, 2)),
            dma((HEADS, 3)), dma((HEADS, 3)),
            dma((HEADS, 3)), dma((HEADS, 3)),
            dma((HEADS, 3, 2)), dma((HEADS, 3, 2)),
            dma((HEADS, 7)), dma((HEADS, 7)), dma((HEADS,)),
        ],
        compiler_params=pltpu.CompilerParams(
            collective_id=0, has_side_effects=True, vmem_limit_bytes=40 << 20),
    )(valid, cond_query, cond_kv, uncond_qkv)


def on_device(cond_query, cond_kv, uncond_qkv, uncond_cache, refresh, valid):
    tokens = attend(cond_query, cond_kv, uncond_qkv, valid)
    new_cache = jnp.where(refresh[:, None] == 1, tokens[1], uncond_cache)
    chosen = new_cache.astype(jnp.float32)
    guided = (chosen + GUIDANCE * (tokens[0].astype(jnp.float32) - chosen)).astype(jnp.bfloat16)
    return (guided, new_cache)


def solution(mesh):
    placed = (
        P("blk", "uly"),
        P(None, "blk", "uly"),
        P(None, ("blk", "uly"), None),
        P(("blk", "uly"), None),
        P(("blk", "uly")),
        P(),
    )
    return jax.shard_map(
        on_device,
        mesh=mesh,
        in_specs=placed,
        out_specs=(P(("blk", "uly"), None), P(("blk", "uly"), None)),
        check_vma=False,
    )
```

time: 1210 us -> 83.5 us (0.07)
  waiting for transfers between devices: 846 us -> 0 us
  other arithmetic: 96.5 us -> 1.64 us
  local copies, waits for them, and re-layouts: 91.6 us -> 3.1 us
  starting transfers between devices: 84.7 us -> 0 us
  matrix products: 84 us -> 0 us
  Pallas kernels: 0 us -> 77.9 us
    ppermute x62 -> x0, waiting for transfers between devices: 835 us -> none  [shifted(): return lax.ppermute(block, axis, route)]
    dot_general x128 -> x0, matrix products: 84 us -> none  [the longest x64 46.6 us: absorb_range(): jnp.einsum('qhd,khd->hqk', query_heads, key_heads, preferred_element_type...]
    all_to_all x3 -> x0, starting transfers between devices: 78.4 us -> none  [the longest x1 36.5 us: on_device(): lax.all_to_all(fresh, 'uly', split_axis=0, concat_axis=1, tiled=True)]
    pallas_call x0 -> x1, Pallas kernels: none -> 77.9 us  [attend(): pl.pallas_call(kernel, out_shape=jax.ShapeDtypeStruct((2, PIECE, 4 * HEAD...]
    lt x63 -> x0, other arithmetic: 59.4 us -> none  [counted(): return jnp.arange(key_rows, dtype=jnp.int32) < valid_count]
    dynamic_slice x63 -> x0, local copies, waits for them, and re-layouts: 39.1 us -> none  [the longest x62 38.5 us: step_forward(): held = update(held, queries, moving, valid[(position - offset) % shards])]
    reduce_sum x63 -> x0, other arithmetic: 33.9 us -> none  [absorb_range(): denominator = denominator * rescale + jnp.sum(weights, axis=2)]
    slice x195 -> x0, local copies, waits for them, and re-layouts: 28.9 us -> none  [the longest x128 16.3 us: absorb_range(): value_heads = kv_block[1].reshape(key_rows, groups, HD)]
  transfers between devices with their start and end apart: 65 -> 0, of which waited for: 64 -> 0; matrix products, arithmetic and copies ran while one was open for 13% -> 0% of each run, Pallas kernels for 0% -> 0%
where the time goes in v1:
time: 83.5 us; the launch traced here: 83.3 us
  Pallas kernels  77.9 us (93%)
  local copies, waits for them, and re-layouts  3.1 us (4%)
  other arithmetic  1.64 us (2%)
    pallas_call x1, Pallas kernels, attend(): pl.pallas_call(kernel, out_shape=jax.ShapeDtypeStruct((2, PIECE, 4 * HEAD...  77.9 us
    unnamed x10, local copies, waits for them, and re-layouts  3.1 us

profile of v1, /device:TPU:1, one launch (start us, length us, event | category | flops | bytes accessed | tf_op | source)
XLA Modules:
  0.0 83.3 jit_solution(4129526253333001967)
XLA Ops:
  0.6 0.0 copy-start.3
  0.6 0.7 broadcast_compare_fusion
  1.3 0.0 copy-done.3
  1.3 0.0 copy-start
  1.3 1.1 %copy-done = bf16[3,48,2560]{2,1,0:T(8,128)(2,1)S(1)} copy-done((bf16[3,48,2560]{2,1,0:T(8,128)(2,1)S(1)}, bf16[3,48,2560]{2,1,0:T(8,128)(2,1)}, u32[]{:S(2)}) %copy-start) | copy-done | bytes 737304
  2.4 0.0 copy-start.1
  2.4 1.0 %copy-done.1 = bf16[2,192,640]{2,1,0:T(8,128)(2,1)S(1)} copy-done((bf16[2,192,640]{2,1,0:T(8,128)(2,1)S(1)}, bf16[2,192,640]{2,1,0:T(8,128)(2,1)}, u32[]{:S(2)}) %copy-start.1) | copy-done | bytes 491544
  3.5 0.0 copy-start.2
  3.5 0.9 %copy-done.2 = bf16[192,640]{1,0:T(8,128)(2,1)S(1)} copy-done((bf16[192,640]{1,0:T(8,128)(2,1)S(1)}, bf16[192,640]{1,0:T(8,128)(2,1)}, u32[]{:S(2)}) %copy-start.2) | copy-done | bytes 245784
  4.4 0.0 copy-start.4
  4.4 77.9 %shard_map.77 = bf16[2,48,2560]{2,1,0:T(8,128)(2,1)S(1)} custom-call(s32[32]{0:T(128)S(1)} %copy-done.3, bf16[192,640]{1,0:T(8,128)(2,1)S(1)} %copy-done.2, bf16[2,192,640]{2,1,0:T(8,128)(2,1)S(1)} %copy-done.1, bf16[3,48,2560]{2,1,0:T(8,128)(2,1)S(1)} %copy-done), custom_call_target="tpu_custom_call" | custom-call | tf_op jit(solution)/shard_map/pallas_call | solution.py:313
  82.3 0.0 copy-done.4
  82.3 1.0 %fusion.1 = (bf16[48,2560]{1,0:T(8,128)(2,1)}, bf16[48,2560]{1,0:T(8,128)(2,1)}) fusion(bf16[2,48,2560]{2,1,0:T(8,128)(2,1)S(1)} %shard_map.77, bf16[48,2560]{1,0:T(8,128)(2,1)S(1)} %copy-done.4, pred[48]{0:T(512)(128)(4,1)S(1)} %broadcast_compare_fusion), kind=kLoop, calls=%fused_computation.3 | loop fusion | flops 860160 | bytes 1228848 | tf_op jit(solution)/shard_map/convert_element_type | solution.py:345
Async XLA Ops:
  0.6 0.7 copy-start.3
  1.3 1.1 %copy-start = (bf16[3,48,2560]{2,1,0:T(8,128)(2,1)S(1)}, bf16[3,48,2560]{2,1,0:T(8,128)(2,1)}, u32[]{:S(2)}) copy-start(bf16[3,48,2560]{2,1,0:T(8,128)(2,1)} %qkv_hbm.1) | copy-start | bytes 2211844
  2.4 1.0 %copy-start.1 = (bf16[2,192,640]{2,1,0:T(8,128)(2,1)S(1)}, bf16[2,192,640]{2,1,0:T(8,128)(2,1)}, u32[]{:S(2)}) copy-start(bf16[2,192,640]{2,1,0:T(8,128)(2,1)} %kv_hbm.1) | copy-start | bytes 1474564
  3.5 0.9 %copy-start.2 = (bf16[192,640]{1,0:T(8,128)(2,1)S(1)}, bf16[192,640]{1,0:T(8,128)(2,1)}, u32[]{:S(2)}) copy-start(bf16[192,640]{1,0:T(8,128)(2,1)} %q_hbm.1) | copy-start | bytes 737284
  4.4 77.9 %copy-start.4 = (bf16[48,2560]{1,0:T(8,128)(2,1)S(1)}, bf16[48,2560]{1,0:T(8,128)(2,1)}, u32[]{:S(2)}) copy-start(bf16[48,2560]{1,0:T(8,128)(2,1)} %param.9) | copy-start | bytes 737284

commit v2 on v0

v2 whole, which is shorter than its diff:
```python
import functools

import jax
import jax.numpy as jnp
from jax import lax
from jax.experimental import pallas as pl
from jax.experimental.pallas import tpu as pltpu
from jax.sharding import PartitionSpec as P

HD = 128
GUIDANCE = 5.0
MESH = pl.DeviceIdType.MESH
LOG2E = 1.4426950408889634
SCALE = LOG2E * HD ** (-0.5)
UNUSABLE = -1e30

HALF = HD // 2
HEADS = 5
LAST = HEADS - 1
WIDTH = HEADS * HD
UNITS = ((0, 1), (1, 1), (2, 1), (3, 2))
SHARD = 192
PIECE = 48
PAIR = 2 * SHARD
ALL = 4 * PAIR
TILE = 256
NT = (((1,), (1,)), ((), ()))
STEPS = (0, 3, 2, 1)


def slot_rows(slot):
    return pl.ds(slot * PAIR, PAIR)


def head_lanes(head):
    return pl.ds(pl.multiple_of(head * HD, HD), HD)


def kernel(
    valid_ref, q_hbm, kv_hbm, qkv_hbm, cache_ref, refresh_ref, guided_out, cache_out,
    qkv, vt, bias, ones, scores_even, scores_odd, partial, tops, stats,
    o_send, st_send, o_half_in, st_half_in, o_full, o_full_in, st_full, st_full_in, o_recv, st_recv, stage, tokens,
    y_sem, g_sem, o_sem, d_sem, f_sem, y_sent, g_sent, o_sent, d_sent, f_sent,
):
    blk, uly = lax.axis_index("blk"), lax.axis_index("uly")
    hi, x, z = blk // 16, (blk // 4) % 4, blk % 4
    me = hi * 4 + uly
    role = lax.rem(hi + uly // 2, 2)

    def column(member):
        return ((member // 4) * 16 + x * 4 + z, member % 4)

    def along_x(step):
        return (hi * 16 + lax.rem(x + step, 4) * 4 + z, uly)

    def along_z(step):
        return (hi * 16 + x * 4 + lax.rem(z + step, 4), uly)

    def remote(src, dst, sent, arrived, to):
        return pltpu.make_async_remote_copy(src, dst, sent, arrived, device_id=to, device_id_type=MESH)

    def wait_for(ref, sem):
        pltpu.make_async_copy(ref, ref, sem).wait()

    barrier = pltpu.get_barrier_semaphore()
    for step in range(1, 8):
        pl.semaphore_signal(barrier, inc=1, device_id=column(lax.rem(me + step, 8)), device_id_type=MESH)
    for step in (1, 2, 3):
        pl.semaphore_signal(barrier, inc=1, device_id=along_z(step), device_id_type=MESH)
    for step in (1, 3):
        pl.semaphore_signal(barrier, inc=1, device_id=along_x(step), device_id_type=MESH)

    def unit_lanes(unit, group=None):
        first, count = UNITS[unit]
        if group is None:
            return pl.ds(first * HD, count * HD)
        return pl.ds(pl.multiple_of(group * WIDTH + first * HD, HD), count * HD)

    def y_start(unit):
        lanes = unit_lanes(unit)
        rows = pl.ds(pl.multiple_of(hi * SHARD, SHARD), SHARD)
        cond = (
            (q_hbm.at[:, lanes], qkv.at[0, rows, lanes]),
            (kv_hbm.at[:, :, lanes], qkv.at[pl.ds(1, 2), rows, lanes]))
        piece = qkv.at[:, pl.ds(pl.multiple_of(me * PIECE, PIECE), PIECE), lanes]

        @pl.when(role == 0)
        def _():
            for src, dst in cond:
                pltpu.make_async_copy(src, dst, y_sem.at[unit]).start()

        @pl.when(role == 1)
        def _():
            for src, dst in cond:
                remote(src, dst, y_sent, y_sem.at[unit], column((uly // 2) * 4 + uly)).start()
            pltpu.make_async_copy(qkv_hbm.at[:, :, unit_lanes(unit, uly)], piece, y_sem.at[unit]).start()

        for group in range(4):
            owner = (1 - group // 2) * 4 + group

            @pl.when(me != owner)
            def _():
                remote(qkv_hbm.at[:, :, unit_lanes(unit, group)], piece, y_sent, y_sem.at[unit], column(owner)).start()

    def y_wait(unit):
        wait_for(qkv.at[:, slot_rows(0), unit_lanes(unit)], y_sem.at[unit])

    def y_settle():
        @pl.when(role == 0)
        def _():
            wait_for(qkv.at[:, pl.ds(0, SHARD), :], y_sent)

        @pl.when(role == 1)
        def _():
            wait_for(qkv.at[:, pl.ds(0, PAIR - PIECE), :], y_sent)

    def gathered(kind, head, rows):
        return qkv.at[0 if kind == 0 else pl.ds(1, 2), rows, head_lanes(head)]

    def gather(kind, head, order):
        for step, slot, row in ((1, 1, 0), (3, 3, SHARD)):
            if order == 0:
                src, dst = slot_rows(0), slot_rows(slot)
            else:
                src, dst = pl.ds(slot * PAIR + row, SHARD), pl.ds(2 * PAIR + row, SHARD)
            remote(
                gathered(kind, head, src), gathered(kind, head, dst), g_sent.at[kind], g_sem.at[head, kind, order],
                along_z(step) if kind == 0 else along_x(step)).start()

    def gather_wait(kind, head, order):
        wait_for(gathered(kind, head, pl.ds(0, (2 - order) * PAIR)), g_sem.at[head, kind, order])

    def direct(slot):
        to = along_z(STEPS[slot])
        into = STEPS[slot] - 1
        remote(o_send.at[LAST, :, slot_rows(slot)], o_recv.at[into], d_sent.at[0], d_sem.at[0], to).start()
        remote(st_send.at[LAST, slot], st_recv.at[into], d_sent.at[1], d_sem.at[1], to).start()

    def hand_over(head, stage_of):
        for side, step in ((0, 1), (1, 3)):
            if stage_of == 0:
                data = (o_send.at[head, pl.ds(side * HALF, HALF), slot_rows(2)], o_half_in.at[head, side])
                note = (st_send.at[head, 2], st_half_in.at[head, side])
            else:
                data = (o_full.at[head, side], o_full_in.at[head, side])
                note = (st_full.at[head, side], st_full_in.at[head, side])
            for i, (src, dst) in enumerate((data, note)):
                remote(src, dst, o_sent.at[stage_of, i], o_sem.at[head, stage_of, i], along_z(step)).start()

    def give_back(first, count):
        src_lanes = pl.ds(first * HD, count * HD)
        dst_lanes = pl.ds(pl.multiple_of(uly * WIDTH + first * HD, HD), count * HD)

        def refs(target):
            rows = pl.ds(pl.multiple_of(target * PIECE, PIECE), PIECE)
            return stage.at[rows, src_lanes], tokens.at[role, :, dst_lanes]

        for step in range(1, 8):
            target = lax.rem(me + step, 8)
            src, dst = refs(target)
            remote(src, dst, f_sent, f_sem, column(target)).start()
        src, dst = refs(me)
        pltpu.make_async_copy(src, dst, f_sem).start()

    def prepare():
        lane = lax.broadcasted_iota(jnp.int32, (SHARD, HD), 1)
        row = lax.broadcasted_iota(jnp.int32, (SHARD, HD), 0)
        for slot in range(4):
            for half in range(2):
                present = valid_ref[half * 16 + lax.rem(x + 4 - slot, 4) * 4 + z]
                block = jnp.where((row >= present) & (lane == 0), UNUSABLE, 0.0)
                bias[pl.ds(slot * PAIR + half * SHARD, SHARD), :] = block.astype(jnp.bfloat16)
        ones[...] = jnp.where(
            lax.broadcasted_iota(jnp.int32, (TILE, HD), 1) == 0, 1.0, 0.0).astype(jnp.bfloat16)
        vt[pl.ds(HD, 16), :] = jnp.ones((16, ALL), jnp.bfloat16)

    def transpose_values(head, slots):
        rows = lax.broadcasted_iota(jnp.int32, (HD, HD), 0)
        lanes = lax.broadcasted_iota(jnp.int32, (HD, HD), 1)
        eye = (rows == lanes).astype(jnp.bfloat16)
        for slot in slots:
            vt[pl.ds(0, HD), slot_rows(slot)] = lax.dot_general(
                eye, qkv[2, slot_rows(slot), head_lanes(head)], NT,
                preferred_element_type=jnp.float32).astype(jnp.bfloat16)

    def attend_slots(head, slots, combine, store):
        buffers = (scores_even, scores_odd)
        starts = [i * TILE for i in (3, 4, 5, 2, 1, 0)]

        def scored(i, k):
            queries = jnp.concatenate([qkv[0, pl.ds(starts[i], TILE), head_lanes(head)], ones[...]], axis=1)
            keys = jnp.concatenate([qkv[1, slot_rows(slots[k]), head_lanes(head)], bias[slot_rows(slots[k]), :]], axis=1)
            part = lax.dot_general(keys, queries, NT, preferred_element_type=jnp.float32)
            buffers[i % 2][slot_rows(k), :] = part
            return jnp.max(part.reshape(PAIR // 8, 8, TILE), axis=0)

        def weighted(i, k, top):
            weights = jnp.exp2((buffers[i % 2][slot_rows(k), :] - top) * SCALE).astype(jnp.bfloat16)
            return jnp.dot(vt[:, slot_rows(slots[k])], weights, preferred_element_type=jnp.float32)

        def whole(parts):
            return jnp.max(functools.reduce(jnp.maximum, parts), axis=0, keepdims=True)

        top = whole([scored(0, k) for k in range(len(slots))])
        for i, start in enumerate(starts):
            lanes = pl.ds(start, TILE)
            top = combine(lanes, top)
            total, next_tops = None, []
            for k in range(len(slots)):
                if i + 1 < len(starts):
                    next_tops.append(scored(i + 1, k))
                part = weighted(i, k, top)
                total = part if total is None else total + part
            store(i, lanes, top, total)
            if next_tops:
                top = whole(next_tops)

    def packed(top, total):
        rows = [row[:, i * HD:(i + 1) * HD] for row in (top, total) for i in range(3)]
        return jnp.concatenate(rows + [jnp.zeros((2, HD), jnp.float32)], axis=0)

    def unpacked(block):
        return tuple(
            jnp.concatenate([block[k + i:k + i + 1] for i in range(3)], axis=1) for k in (0, 3))

    def near_keys(head):
        transpose_values(head, (0, 1, 3))

        def store(i, lanes, top, total):
            partial[:, lanes] = total
            tops[:, lanes] = top

        attend_slots(head, (0, 1, 3), lambda lanes, top: top, store)

    def far_keys(head):
        transpose_values(head, (2,))

        def combine(lanes, top):
            return jnp.maximum(top, tops[:, lanes])

        def store(i, lanes, top, total):
            total = total + partial[:, lanes] * jnp.exp2((tops[:, lanes] - top) * SCALE)
            o_send[head, :, lanes] = total[:HD].astype(jnp.bfloat16)
            stats[pl.ds(0, 1), lanes] = top
            stats[pl.ds(1, 1), lanes] = total[HD:HD + 1]
            slot = {1: 2, 2: 3, 4: 1, 5: 0}.get(i)
            if slot is not None:
                st_send[head, slot] = packed(
                    stats[pl.ds(0, 1), slot_rows(slot)], stats[pl.ds(1, 1), slot_rows(slot)])
            if slot == 2:
                @pl.when(head < LAST)
                def _():
                    hand_over(head, 0)
            if slot:
                @pl.when(head == LAST)
                def _():
                    direct(slot)

        attend_slots(head, (2,), combine, store)

    def pass_on(head):
        wait_for(o_half_in.at[head], o_sem.at[head, 0, 0])
        wait_for(st_half_in.at[head], o_sem.at[head, 0, 1])
        for side, slot in ((0, 3), (1, 1)):
            own_top, own_sum = unpacked(st_send[head, slot])
            in_top, in_sum = unpacked(st_half_in[head, side])
            top = jnp.maximum(own_top, in_top)
            own_factor, in_factor = jnp.exp2((own_top - top) * SCALE), jnp.exp2((in_top - top) * SCALE)
            for half in range(2):
                rows = pl.ds(half * HALF, HALF)
                block = o_send[head, rows, slot_rows(slot)].astype(jnp.float32) * own_factor
                if half == side:
                    block = block + o_half_in[head, side].astype(jnp.float32) * in_factor
                o_full[head, side, rows] = block.astype(jnp.bfloat16)
            total = own_sum * own_factor
            if side == 0:
                total = total + in_sum * in_factor
            st_full[head, side] = packed(top, total)
        hand_over(head, 1)

    def merge(head):
        if isinstance(head, int) and head == LAST:
            wait_for(o_recv, d_sem.at[0])
            wait_for(st_recv, d_sem.at[1])
            arrived = [(o_recv[i], st_recv[i]) for i in range(3)]
        else:
            wait_for(o_full_in.at[head], o_sem.at[head, 1, 0])
            wait_for(st_full_in.at[head], o_sem.at[head, 1, 1])
            arrived = [(o_full_in[head, side], st_full_in[head, side]) for side in range(2)]
        arrived.append((o_send[head, :, slot_rows(0)], st_send[head, 0]))
        pairs = [unpacked(block) for _, block in arrived]
        top = functools.reduce(jnp.maximum, [pair[0] for pair in pairs])
        factors = [jnp.exp2((pair[0] - top) * SCALE) for pair in pairs]
        denominator = sum(f * pair[1] for f, pair in zip(factors, pairs))
        numerator = sum(f * block.astype(jnp.float32) for f, (block, _) in zip(factors, arrived))
        stage[:, head_lanes(head)] = (numerator / denominator).T.astype(jnp.bfloat16)

    def spread(head):
        for kind in range(2):
            gather(kind, head, 0)

    def relay(head):
        for kind in range(2):
            gather_wait(kind, head, 0)
            gather(kind, head, 1)

    def head_step(head, _):
        gather_wait(0, head, 1)
        near_keys(head)

        @pl.when(head < LAST)
        def _():
            relay(head + 1)

        @pl.when(head >= 1)
        def _():
            pass_on(head - 1)

        gather_wait(1, head, 1)
        far_keys(head)

        @pl.when(head == 0)
        def _():
            y_wait(3)

        @pl.when(head + 3 < HEADS)
        def _():
            spread(head + 3)

        @pl.when(head >= 2)
        def _():
            merge(head - 2)

        return 0

    pl.semaphore_wait(barrier, 12)
    y_start(0)
    y_start(1)
    prepare()
    y_wait(0)
    spread(0)
    y_start(2)
    y_wait(1)
    spread(1)
    y_start(3)
    relay(0)
    y_wait(2)
    spread(2)
    lax.fori_loop(0, HEADS, head_step, 0)
    merge(LAST - 1)
    give_back(0, LAST)
    y_settle()
    wait_for(qkv.at[0, pl.ds(0, 3 * PAIR), :], g_sent.at[0])
    wait_for(qkv.at[pl.ds(1, 2), pl.ds(0, 3 * PAIR), :], g_sent.at[1])
    for i, (data, note) in enumerate(((o_half_in, st_half_in), (o_full, st_full))):
        wait_for(data, o_sent.at[i, 0])
        wait_for(note, o_sent.at[i, 1])
    merge(LAST)
    give_back(LAST, 1)
    wait_for(o_recv, d_sent.at[0])
    wait_for(st_recv, d_sent.at[1])
    lanes = lax.broadcasted_iota(jnp.int32, (PIECE, PIECE), 1)
    rows = lax.broadcasted_iota(jnp.int32, (PIECE, PIECE), 0)
    chosen = jnp.where((rows == lanes) & (refresh_ref[...] == 1), 1.0, 0.0).astype(jnp.bfloat16)
    renew = jnp.dot(chosen, jnp.ones((PIECE, HD), jnp.bfloat16), preferred_element_type=jnp.float32) > 0.5
    wait_for(stage.at[pl.ds(0, PAIR - PIECE), :], f_sent)
    wait_for(tokens, f_sem)
    for block in range(4 * HEADS):
        columns = pl.ds(block * HD, HD)
        kept = cache_ref[:, columns].astype(jnp.float32)
        kept = jnp.where(renew, tokens[1, :, columns].astype(jnp.float32), kept)
        cache_out[:, columns] = kept.astype(jnp.bfloat16)
        guided = kept + GUIDANCE * (tokens[0, :, columns].astype(jnp.float32) - kept)
        guided_out[:, columns] = guided.astype(jnp.bfloat16)


def on_device(cond_query, cond_kv, uncond_qkv, uncond_cache, refresh, valid):
    any_space = pl.BlockSpec(memory_space=pl.ANY)
    vmem = pl.BlockSpec(memory_space=pltpu.VMEM)
    dma = pltpu.SemaphoreType.DMA
    bf16, f32 = jnp.bfloat16, jnp.float32
    result = jax.ShapeDtypeStruct((PIECE, 4 * WIDTH), bf16)
    return pl.pallas_call(
        kernel,
        out_shape=(result, result),
        in_specs=[pl.BlockSpec(memory_space=pltpu.SMEM), any_space, any_space, any_space, vmem, vmem],
        out_specs=(vmem, vmem),
        scratch_shapes=[
            pltpu.VMEM((3, ALL, WIDTH), bf16),
            pltpu.VMEM((HD + 16, ALL), bf16),
            pltpu.VMEM((ALL, HD), bf16),
            pltpu.VMEM((TILE, HD), bf16),
            pltpu.VMEM((3 * PAIR, TILE), f32),
            pltpu.VMEM((3 * PAIR, TILE), f32),
            pltpu.VMEM((HD + 16, ALL), f32),
            pltpu.VMEM((1, ALL), f32),
            pltpu.VMEM((8, ALL), f32),
            pltpu.VMEM((HEADS, HD, ALL), bf16),
            pltpu.VMEM((HEADS, 4, 8, HD), f32),
            pltpu.VMEM((LAST, 2, HALF, PAIR), bf16),
            pltpu.VMEM((LAST, 2, 8, HD), f32),
            pltpu.VMEM((LAST, 2, HD, PAIR), bf16),
            pltpu.VMEM((LAST, 2, HD, PAIR), bf16),
            pltpu.VMEM((LAST, 2, 8, HD), f32),
            pltpu.VMEM((LAST, 2, 8, HD), f32),
            pltpu.VMEM((3, HD, PAIR), bf16),
            pltpu.VMEM((3, 8, HD), f32),
            pltpu.VMEM((PAIR, WIDTH), bf16),
            pltpu.VMEM((2, PIECE, 4 * WIDTH), bf16),
            dma((len(UNITS),)), dma((HEADS, 2, 2)), dma((LAST, 2, 2)), dma((2,)), dma,
            dma, dma((2,)), dma((2, 2)), dma((2,)), dma,
        ],
        compiler_params=pltpu.CompilerParams(
            collective_id=0, has_side_effects=True, vmem_limit_bytes=60 << 20),
    )(valid, cond_query, cond_kv, uncond_qkv, uncond_cache, refresh.reshape(1, PIECE))


def solution(mesh):
    placed = (
        P("blk", "uly"),
        P(None, "blk", "uly"),
        P(None, ("blk", "uly"), None),
        P(("blk", "uly"), None),
        P(("blk", "uly")),
        P(),
    )
    return jax.shard_map(
        on_device,
        mesh=mesh,
        in_specs=placed,
        out_specs=(P(("blk", "uly"), None), P(("blk", "uly"), None)),
        check_vma=False,
    )
```

time: 1210 us -> 70.4 us (0.06)
  waiting for transfers between devices: 846 us -> 0 us
  other arithmetic: 96.5 us -> 0 us
  local copies, waits for them, and re-layouts: 91.6 us -> 2.39 us
  starting transfers between devices: 84.7 us -> 0 us
  matrix products: 84 us -> 0 us
  Pallas kernels: 0 us -> 67.2 us
    ppermute x62 -> x0, waiting for transfers between devices: 835 us -> none  [shifted(): return lax.ppermute(block, axis, route)]
    dot_general x128 -> x0, matrix products: 84 us -> none  [the longest x64 46.6 us: absorb_range(): jnp.einsum('qhd,khd->hqk', query_heads, key_heads, preferred_element_type...]
    all_to_all x3 -> x0, starting transfers between devices: 78.4 us -> none  [the longest x1 36.5 us: on_device(): lax.all_to_all(fresh, 'uly', split_axis=0, concat_axis=1, tiled=True)]
    pallas_call x0 -> x1, Pallas kernels: none -> 67.2 us  [on_device(): pl.pallas_call(kernel, out_shape=(result, result), in_specs=[pl.BlockSpec...]
    lt x63 -> x0, other arithmetic: 59.4 us -> none  [counted(): return jnp.arange(key_rows, dtype=jnp.int32) < valid_count]
    dynamic_slice x63 -> x0, local copies, waits for them, and re-layouts: 39.1 us -> none  [the longest x62 38.5 us: step_forward(): held = update(held, queries, moving, valid[(position - offset) % shards])]
    reduce_sum x63 -> x0, other arithmetic: 33.9 us -> none  [absorb_range(): denominator = denominator * rescale + jnp.sum(weights, axis=2)]
    slice x195 -> x0, local copies, waits for them, and re-layouts: 28.9 us -> none  [the longest x128 16.3 us: absorb_range(): value_heads = kv_block[1].reshape(key_rows, groups, HD)]
  transfers between devices with their start and end apart: 65 -> 0, of which waited for: 64 -> 0; matrix products, arithmetic and copies ran while one was open for 13% -> 0% of each run, Pallas kernels for 0% -> 0%
where the time goes in v2:
time: 70.4 us; the launch traced here: 70.3 us
  Pallas kernels  67.2 us (95%)
  local copies, waits for them, and re-layouts  2.39 us (3%)
    pallas_call x1, Pallas kernels, on_device(): pl.pallas_call(kernel, out_shape=(result, result), in_specs=[pl.BlockSpec...  67.2 us
    unnamed x4, local copies, waits for them, and re-layouts  2.39 us

profile of v2, /device:TPU:1, one launch (start us, length us, event | category | flops | bytes accessed | tf_op | source)
XLA Modules:
  0.0 70.3 jit_solution(14813723373559438414)
XLA Ops:
  0.6 67.2 %shard_map.77 = (bf16[48,2560]{1,0:T(8,128)(2,1)}, bf16[48,2560]{1,0:T(8,128)(2,1)}) custom-call(s32[32]{0:T(128)} %valid_ref.1, bf16[192,640]{1,0:T(8,128)(2,1)} %q_hbm.1, bf16[2,192,640]{2,1,0:T(8,128)(2,1)} %kv_hbm.1, bf16[3,48,2560]{2,1,0:T(8,128)(2,1)} %qkv_hbm.1, bf16[48,2560]{1,0:T(8,128)(2,1)} %cache_ref.1, s32[1,48]{1,0:T(1,128)} %bitcast.1), custom_call_target="tpu_custom_call" | custom-call | tf_op jit(solution)/shard_map/pallas_call | solution.py:383
  67.9 0.0 copy-start
  67.9 1.7 %copy.10 = bf16[48,2560]{1,0:T(8,128)(2,1)} copy(bf16[48,2560]{1,0:T(8,128)(2,1)} %get-tuple-element.4) | data formatting | bytes 491520
  69.6 0.0 copy-done
  69.6 0.7 copy.11
Async XLA Ops:
  67.9 1.7 %copy-start = (bf16[48,2560]{1,0:T(8,128)(2,1)S(1)}, bf16[48,2560]{1,0:T(8,128)(2,1)}, u32[]{:S(2)}) copy-start(bf16[48,2560]{1,0:T(8,128)(2,1)} %get-tuple-element.5) | copy-start | bytes 737284

commit v3 on v2

--- a/solution.py
+++ b/solution.py
@@ -18,7 +18,7 @@
 HEADS = 5
 LAST = HEADS - 1
 WIDTH = HEADS * HD
-UNITS = ((0, 1), (1, 1), (2, 1), (3, 2))
+UNITS = ((1, 1, 0, 1), (2, 1, 0, 1), (0, 1, 0, 1), (0, 3, 1, 1), (0, 3, 2, 1), (0, 3, 3, 2))
 SHARD = 192
 PIECE = 48
 PAIR = 2 * SHARD
@@ -71,7 +71,7 @@
         pl.semaphore_signal(barrier, inc=1, device_id=along_x(step), device_id_type=MESH)
 
     def unit_lanes(unit, group=None):
-        first, count = UNITS[unit]
+        first, count = UNITS[unit][2:]
         if group is None:
             return pl.ds(first * HD, count * HD)
         return pl.ds(pl.multiple_of(group * WIDTH + first * HD, HD), count * HD)
@@ -79,10 +79,16 @@
     def y_start(unit):
         lanes = unit_lanes(unit)
         rows = pl.ds(pl.multiple_of(hi * SHARD, SHARD), SHARD)
-        cond = (
-            (q_hbm.at[:, lanes], qkv.at[0, rows, lanes]),
-            (kv_hbm.at[:, :, lanes], qkv.at[pl.ds(1, 2), rows, lanes]))
-        piece = qkv.at[:, pl.ds(pl.multiple_of(me * PIECE, PIECE), PIECE), lanes]
+        first, count = UNITS[unit][:2]
+        cond = []
+        if first == 0:
+            cond.append((q_hbm.at[:, lanes], qkv.at[0, rows, lanes]))
+        if first + count > 1:
+            low = max(first, 1)
+            span = first + count - low
+            cond.append((kv_hbm.at[pl.ds(low - 1, span), :, lanes], qkv.at[pl.ds(low, span), rows, lanes]))
+        arrays = pl.ds(first, count)
+        piece = qkv.at[arrays, pl.ds(pl.multiple_of(me * PIECE, PIECE), PIECE), lanes]
 
         @pl.when(role == 0)
         def _():
@@ -93,17 +99,19 @@
         def _():
             for src, dst in cond:
                 remote(src, dst, y_sent, y_sem.at[unit], column((uly // 2) * 4 + uly)).start()
-            pltpu.make_async_copy(qkv_hbm.at[:, :, unit_lanes(unit, uly)], piece, y_sem.at[unit]).start()
+            pltpu.make_async_copy(qkv_hbm.at[arrays, :, unit_lanes(unit, uly)], piece, y_sem.at[unit]).start()
 
         for group in range(4):
             owner = (1 - group // 2) * 4 + group
 
             @pl.when(me != owner)
             def _():
-                remote(qkv_hbm.at[:, :, unit_lanes(unit, group)], piece, y_sent, y_sem.at[unit], column(owner)).start()
+                remote(
+                    qkv_hbm.at[arrays, :, unit_lanes(unit, group)], piece, y_sent, y_sem.at[unit],
+                    column(owner)).start()
 
     def y_wait(unit):
-        wait_for(qkv.at[:, slot_rows(0), unit_lanes(unit)], y_sem.at[unit])
+        wait_for(qkv.at[pl.ds(*UNITS[unit][:2]), slot_rows(0), unit_lanes(unit)], y_sem.at[unit])
 
     def y_settle():
         @pl.when(role == 0)
@@ -114,18 +122,18 @@
         def _():
             wait_for(qkv.at[:, pl.ds(0, PAIR - PIECE), :], y_sent)
 
-    def gathered(kind, head, rows):
-        return qkv.at[0 if kind == 0 else pl.ds(1, 2), rows, head_lanes(head)]
-
-    def gather(kind, head, order):
+    def gathered(kind, head, rows, arrays=None):
+        return qkv.at[0 if kind == 0 else pl.ds(1, 2) if arrays is None else arrays, rows, head_lanes(head)]
+
+    def gather(kind, head, order, arrays=None):
         for step, slot, row in ((1, 1, 0), (3, 3, SHARD)):
             if order == 0:
                 src, dst = slot_rows(0), slot_rows(slot)
             else:
                 src, dst = pl.ds(slot * PAIR + row, SHARD), pl.ds(2 * PAIR + row, SHARD)
             remote(
-                gathered(kind, head, src), gathered(kind, head, dst), g_sent.at[kind], g_sem.at[head, kind, order],
-                along_z(step) if kind == 0 else along_x(step)).start()
+                gathered(kind, head, src, arrays), gathered(kind, head, dst, arrays), g_sent.at[kind],
+                g_sem.at[head, kind, order], along_z(step) if kind == 0 else along_x(step)).start()
 
     def gather_wait(kind, head, order):
         wait_for(gathered(kind, head, pl.ds(0, (2 - order) * PAIR)), g_sem.at[head, kind, order])
@@ -321,7 +329,7 @@
 
         @pl.when(head == 0)
         def _():
-            y_wait(3)
+            y_wait(5)
 
         @pl.when(head + 3 < HEADS)
         def _():
@@ -331,24 +339,34 @@
         def _():
             merge(head - 2)
 
+        @pl.when(head == 3)
+        def _():
+            give_back(0, 2)
+
+        @pl.when(head == 4)
+        def _():
+            give_back(2, 1)
+
         return 0
 
     pl.semaphore_wait(barrier, 12)
-    y_start(0)
-    y_start(1)
+    for unit in range(len(UNITS)):
+        y_start(unit)
     prepare()
     y_wait(0)
-    spread(0)
-    y_start(2)
+    gather(1, 0, 0, 1)
     y_wait(1)
+    gather(1, 0, 0, 2)
+    y_wait(2)
+    gather(0, 0, 0)
+    y_wait(3)
     spread(1)
-    y_start(3)
     relay(0)
-    y_wait(2)
+    y_wait(4)
     spread(2)
     lax.fori_loop(0, HEADS, head_step, 0)
     merge(LAST - 1)
-    give_back(0, LAST)
+    give_back(3, 1)
     y_settle()
     wait_for(qkv.at[0, pl.ds(0, 3 * PAIR), :], g_sent.at[0])
     wait_for(qkv.at[pl.ds(1, 2), pl.ds(0, 3 * PAIR), :], g_sent.at[1])

time: 70.4 us -> 67.6 us (0.960)
  Pallas kernels: 67.2 us -> 64.4 us
    pallas_call x1, Pallas kernels: 67.2 us -> 64.4 us  [on_device(): pl.pallas_call(kernel, out_shape=(result, result), in_specs=[pl.BlockSpec...]
where the time goes in v3:
time: 67.6 us; the launch traced here: 67.5 us
  Pallas kernels  64.4 us (95%)
  local copies, waits for them, and re-layouts  2.39 us (4%)
    pallas_call x1, Pallas kernels, on_device(): pl.pallas_call(kernel, out_shape=(result, result), in_specs=[pl.BlockSpec...  64.4 us
    unnamed x4, local copies, waits for them, and re-layouts  2.39 us

profile of v3, /device:TPU:1, one launch (start us, length us, event | category | flops | bytes accessed | tf_op | source)
XLA Modules:
  0.0 67.5 jit_solution(13802946842400463374)
XLA Ops:
  0.6 64.4 %shard_map.77 = (bf16[48,2560]{1,0:T(8,128)(2,1)}, bf16[48,2560]{1,0:T(8,128)(2,1)}) custom-call(s32[32]{0:T(128)} %valid_ref.1, bf16[192,640]{1,0:T(8,128)(2,1)} %q_hbm.1, bf16[2,192,640]{2,1,0:T(8,128)(2,1)} %kv_hbm.1, bf16[3,48,2560]{2,1,0:T(8,128)(2,1)} %qkv_hbm.1, bf16[48,2560]{1,0:T(8,128)(2,1)} %cache_ref.1, s32[1,48]{1,0:T(1,128)} %bitcast.1), custom_call_target="tpu_custom_call" | custom-call | tf_op jit(solution)/shard_map/pallas_call | solution.py:401
  65.1 0.0 copy-start
  65.1 1.7 %copy.10 = bf16[48,2560]{1,0:T(8,128)(2,1)} copy(bf16[48,2560]{1,0:T(8,128)(2,1)} %get-tuple-element.4) | data formatting | bytes 491520
  66.8 0.0 copy-done
  66.8 0.7 %copy.11 = bf16[48,2560]{1,0:T(8,128)(2,1)} copy(bf16[48,2560]{1,0:T(8,128)(2,1)S(1)} %copy-done) | data formatting | bytes 491520
Async XLA Ops:
  65.1 1.7 %copy-start = (bf16[48,2560]{1,0:T(8,128)(2,1)S(1)}, bf16[48,2560]{1,0:T(8,128)(2,1)}, u32[]{:S(2)}) copy-start(bf16[48,2560]{1,0:T(8,128)(2,1)} %get-tuple-element.5) | copy-start | bytes 737284

commit v4 on v3

--- a/solution.py
+++ b/solution.py
@@ -19,6 +19,7 @@
 LAST = HEADS - 1
 WIDTH = HEADS * HD
 UNITS = ((1, 1, 0, 1), (2, 1, 0, 1), (0, 1, 0, 1), (0, 3, 1, 1), (0, 3, 2, 1), (0, 3, 3, 2))
+RETURNS = ((0, 2), (2, 1), (3, 1), (4, 1))
 SHARD = 192
 PIECE = 48
 PAIR = 2 * SHARD
@@ -155,7 +156,8 @@
             for i, (src, dst) in enumerate((data, note)):
                 remote(src, dst, o_sent.at[stage_of, i], o_sem.at[head, stage_of, i], along_z(step)).start()
 
-    def give_back(first, count):
+    def give_back(part):
+        first, count = RETURNS[part]
         src_lanes = pl.ds(first * HD, count * HD)
         dst_lanes = pl.ds(pl.multiple_of(uly * WIDTH + first * HD, HD), count * HD)
 
@@ -166,9 +168,9 @@
         for step in range(1, 8):
             target = lax.rem(me + step, 8)
             src, dst = refs(target)
-            remote(src, dst, f_sent, f_sem, column(target)).start()
+            remote(src, dst, f_sent, f_sem.at[part], column(target)).start()
         src, dst = refs(me)
-        pltpu.make_async_copy(src, dst, f_sem).start()
+        pltpu.make_async_copy(src, dst, f_sem.at[part]).start()
 
     def prepare():
         lane = lax.broadcasted_iota(jnp.int32, (SHARD, HD), 1)
@@ -341,11 +343,11 @@
 
         @pl.when(head == 3)
         def _():
-            give_back(0, 2)
+            give_back(0)
 
         @pl.when(head == 4)
         def _():
-            give_back(2, 1)
+            give_back(1)
 
         return 0
 
@@ -366,7 +368,7 @@
     spread(2)
     lax.fori_loop(0, HEADS, head_step, 0)
     merge(LAST - 1)
-    give_back(3, 1)
+    give_back(2)
     y_settle()
     wait_for(qkv.at[0, pl.ds(0, 3 * PAIR), :], g_sent.at[0])
     wait_for(qkv.at[pl.ds(1, 2), pl.ds(0, 3 * PAIR), :], g_sent.at[1])
@@ -374,22 +376,24 @@
         wait_for(data, o_sent.at[i, 0])
         wait_for(note, o_sent.at[i, 1])
     merge(LAST)
-    give_back(LAST, 1)
-    wait_for(o_recv, d_sent.at[0])
-    wait_for(st_recv, d_sent.at[1])
+    give_back(3)
     lanes = lax.broadcasted_iota(jnp.int32, (PIECE, PIECE), 1)
     rows = lax.broadcasted_iota(jnp.int32, (PIECE, PIECE), 0)
     chosen = jnp.where((rows == lanes) & (refresh_ref[...] == 1), 1.0, 0.0).astype(jnp.bfloat16)
     renew = jnp.dot(chosen, jnp.ones((PIECE, HD), jnp.bfloat16), preferred_element_type=jnp.float32) > 0.5
-    wait_for(stage.at[pl.ds(0, PAIR - PIECE), :], f_sent)
-    wait_for(tokens, f_sem)
-    for block in range(4 * HEADS):
-        columns = pl.ds(block * HD, HD)
-        kept = cache_ref[:, columns].astype(jnp.float32)
-        kept = jnp.where(renew, tokens[1, :, columns].astype(jnp.float32), kept)
-        cache_out[:, columns] = kept.astype(jnp.bfloat16)
-        guided = kept + GUIDANCE * (tokens[0, :, columns].astype(jnp.float32) - kept)
-        guided_out[:, columns] = guided.astype(jnp.bfloat16)
+    for part, (first, count) in enumerate(RETURNS):
+        if part == len(RETURNS) - 1:
+            wait_for(o_recv, d_sent.at[0])
+            wait_for(st_recv, d_sent.at[1])
+            wait_for(stage.at[pl.ds(0, PAIR - PIECE), :], f_sent)
+        wait_for(tokens.at[:, :, pl.ds(0, 4 * count * HD)], f_sem.at[part])
+        for block in (group * HEADS + first + i for group in range(4) for i in range(count)):
+            columns = pl.ds(block * HD, HD)
+            kept = cache_ref[:, columns].astype(jnp.float32)
+            kept = jnp.where(renew, tokens[1, :, columns].astype(jnp.float32), kept)
+            cache_out[:, columns] = kept.astype(jnp.bfloat16)
+            guided = kept + GUIDANCE * (tokens[0, :, columns].astype(jnp.float32) - kept)
+            guided_out[:, columns] = guided.astype(jnp.bfloat16)
 
 
 def on_device(cond_query, cond_kv, uncond_qkv, uncond_cache, refresh, valid):
@@ -425,11 +429,11 @@
             pltpu.VMEM((3, 8, HD), f32),
             pltpu.VMEM((PAIR, WIDTH), bf16),
             pltpu.VMEM((2, PIECE, 4 * WIDTH), bf16),
-            dma((len(UNITS),)), dma((HEADS, 2, 2)), dma((LAST, 2, 2)), dma((2,)), dma,
+            dma((len(UNITS),)), dma((HEADS, 2, 2)), dma((LAST, 2, 2)), dma((2,)), dma((len(RETURNS),)),
             dma, dma((2,)), dma((2, 2)), dma((2,)), dma,
         ],
         compiler_params=pltpu.CompilerParams(
-            collective_id=0, has_side_effects=True, vmem_limit_bytes=60 << 20),
+            collective_id=0, has_side_effects=True, vmem_limit_bytes=54592 << 10)
     )(valid, cond_query, cond_kv, uncond_qkv, uncond_cache, refresh.reshape(1, PIECE))
 
 

time: 67.6 us -> 66.3 us (0.981)
  Pallas kernels: 64.4 us -> 63.5 us
    pallas_call x1, Pallas kernels: 64.4 us -> 63.5 us  [on_device(): pl.pallas_call(kernel, out_shape=(result, result), in_specs=[pl.BlockSpec...]
    unnamed x4 -> x6, local copies, waits for them, and re-layouts: 2.39 us -> 2.04 us
where the time goes in v4:
time: 66.3 us; the launch traced here: 66.2 us
  Pallas kernels  63.5 us (96%)
  local copies, waits for them, and re-layouts  2.04 us (3%)
    pallas_call x1, Pallas kernels, on_device(): pl.pallas_call(kernel, out_shape=(result, result), in_specs=[pl.BlockSpec...  63.5 us
    unnamed x6, local copies, waits for them, and re-layouts  2.04 us

profile of v4, /device:TPU:1, one launch (start us, length us, event | category | flops | bytes accessed | tf_op | source)
XLA Modules:
  0.0 66.2 jit_solution(12315294858736300368)
XLA Ops:
  0.6 0.0 copy-start
  0.6 0.0 copy-start.1
  0.7 0.6 copy-done
  1.3 0.0 copy-done.1
  1.3 63.5 %shard_map.77 = (bf16[48,2560]{1,0:T(8,128)(2,1)S(1)}, bf16[48,2560]{1,0:T(8,128)(2,1)S(1)}) custom-call(s32[32]{0:T(128)S(1)} %copy-done, bf16[192,640]{1,0:T(8,128)(2,1)} %q_hbm.1, bf16[2,192,640]{2,1,0:T(8,128)(2,1)} %kv_hbm.1, bf16[3,48,2560]{2,1,0:T(8,128)(2,1)} %qkv_hbm.1, bf16[48,2560]{1,0:T(8,128)(2,1)} %cache_ref.1, s32[1,48]{1,0:T(1,128)S(1)} %bitcast.1), custom_call_target="tpu_custom_call" | custom-call | tf_op jit(solution)/shard_map/pallas_call | solution.py:405
  64.8 0.7 %copy.10 = bf16[48,2560]{1,0:T(8,128)(2,1)} copy(bf16[48,2560]{1,0:T(8,128)(2,1)S(1)} %get-tuple-element.4) | data formatting | bytes 491520
  65.5 0.7 %copy.11 = bf16[48,2560]{1,0:T(8,128)(2,1)} copy(bf16[48,2560]{1,0:T(8,128)(2,1)S(1)} %get-tuple-element.5) | data formatting | bytes 491520
Async XLA Ops:
  0.6 0.7 copy-start
  0.6 0.7 %copy-start.1 = (s32[48]{0:T(128)S(1)}, s32[48]{0:T(128)}, u32[]{:S(2)}) copy-start(s32[48]{0:T(128)} %param.10) | copy-start | bytes 580

commit v5 on v4

--- a/solution.py
+++ b/solution.py
@@ -18,7 +18,7 @@
 HEADS = 5
 LAST = HEADS - 1
 WIDTH = HEADS * HD
-UNITS = ((1, 1, 0, 1), (2, 1, 0, 1), (0, 1, 0, 1), (0, 3, 1, 1), (0, 3, 2, 1), (0, 3, 3, 2))
+UNITS = ((1, 1, 0, 1), (2, 1, 0, 1), (0, 1, 0, 1), (0, 3, 1, 1), (0, 3, 2, 1), (0, 3, 3, 1), (0, 3, 4, 1))
 RETURNS = ((0, 2), (2, 1), (3, 1), (4, 1))
 SHARD = 192
 PIECE = 48
@@ -329,12 +329,9 @@
         gather_wait(1, head, 1)
         far_keys(head)
 
-        @pl.when(head == 0)
-        def _():
-            y_wait(5)
-
         @pl.when(head + 3 < HEADS)
         def _():
+            wait_for(qkv.at[:, slot_rows(0), head_lanes(head + 3)], y_sem.at[head + 5])
             spread(head + 3)
 
         @pl.when(head >= 2)

time: 66.3 us -> 66.3 us (level)
  no operation moved by 1% of the time
where the time goes in v5:
time: 66.3 us; the launch traced here: 66.2 us
  Pallas kernels  63.5 us (96%)
  local copies, waits for them, and re-layouts  2.04 us (3%)
    pallas_call x1, Pallas kernels, on_device(): pl.pallas_call(kernel, out_shape=(result, result), in_specs=[pl.BlockSpec...  63.5 us
    unnamed x6, local copies, waits for them, and re-layouts  2.04 us

profile of v5, /device:TPU:1, one launch (start us, length us, event | category | flops | bytes accessed | tf_op | source)
XLA Modules:
  0.0 66.2 jit_solution(2289734609313270888)
XLA Ops:
  0.6 0.0 copy-start
  0.6 0.0 copy-start.1
  0.7 0.6 copy-done
  1.3 0.0 copy-done.1
  1.3 63.5 %shard_map.77 = (bf16[48,2560]{1,0:T(8,128)(2,1)S(1)}, bf16[48,2560]{1,0:T(8,128)(2,1)S(1)}) custom-call(s32[32]{0:T(128)S(1)} %copy-done, bf16[192,640]{1,0:T(8,128)(2,1)} %q_hbm.1, bf16[2,192,640]{2,1,0:T(8,128)(2,1)} %kv_hbm.1, bf16[3,48,2560]{2,1,0:T(8,128)(2,1)} %qkv_hbm.1, bf16[48,2560]{1,0:T(8,128)(2,1)} %cache_ref.1, s32[1,48]{1,0:T(1,128)S(1)} %bitcast.1), custom_call_target="tpu_custom_call" | custom-call | tf_op jit(solution)/shard_map/pallas_call | solution.py:402
  64.8 0.7 %copy.10 = bf16[48,2560]{1,0:T(8,128)(2,1)} copy(bf16[48,2560]{1,0:T(8,128)(2,1)S(1)} %get-tuple-element.4) | data formatting | bytes 491520
  65.5 0.7 %copy.11 = bf16[48,2560]{1,0:T(8,128)(2,1)} copy(bf16[48,2560]{1,0:T(8,128)(2,1)S(1)} %get-tuple-element.5) | data formatting | bytes 491520
Async XLA Ops:
  0.6 0.7 copy-start
  0.6 0.7 %copy-start.1 = (s32[48]{0:T(128)S(1)}, s32[48]{0:T(128)}, u32[]{:S(2)}) copy-start(s32[48]{0:T(128)} %param.10) | copy-start | bytes 580
